TPU v7x, 32 devices: a whole 2x2x4 slice. The times are simulated.
32 devices in a mesh: tm: 8 (over y, x, core), tile: 4 (over z).
Axes of the slice: x: 2, y: 2, z: 4, core: 2. Of those that a mesh axis runs over, the one named last changes fastest.
Arguments:
- velocity_u: float32 [384, 2, 16, 1024], P('tm', None, None, 'tile'), may hold values from -12 to 12
- velocity_v: float32 [384, 2, 16, 1024], P('tm', None, None, 'tile'), may hold values from -12 to 12
- land_sea: int32 [16, 1024], P(None, 'tile'), may hold values 0 or 1
- bottom_level: int32 [16, 1024], P(None, 'tile'), may hold values from 0 to 2
- spacing_x: float32 [16, 1024], P(None, 'tile'), may hold values from 0.5 to 2
- spacing_y: float32 [16, 1024], P(None, 'tile'), may hold values from 0.5 to 2
Outputs:
- conversion_maps: bfloat16 [384, 2, 16, 1024], P('tm', None, None, 'tile')
- mean_map: float32 [2, 16, 1024], P(None, None, 'tile')
All inputs are finite; a program needn't handle non-finite values. No bound on the sum of `land_sea` on one device may be relied on, other than what follows from the above.
Results may differ from a plain program's by a relative error of at most 0.001.
Values sent between devices are 32-bit elements; how exact they have to be, the bound alone decides.
A program may use at most 64 MiB of HBM per device.

v0:
```python
import functools

import jax
import jax.numpy as jnp
import numpy as np
from jax import lax
from jax.experimental import pallas as pl
from jax.experimental.pallas import tpu as pltpu
from jax.sharding import PartitionSpec as P

HALF = 24
CUTOFF = 1.0 / 40.0
LANES = 128
CHUNK = 8
DEPTH = 2
UNROLL = 4
MESH = pl.DeviceIdType.MESH


def band_parts(count):
    offset = (np.arange(count + 2 * HALF)[None, :] - np.arange(count)[:, None] - HALF).astype(np.float64)
    weights = 2.0 * CUTOFF * np.sinc(2.0 * CUTOFF * offset) * np.sinc(offset / HALF)
    weights = np.where(np.abs(offset) <= HALF, weights, 0.0).astype(np.float32)
    own = weights[:, HALF : HALF + count]
    halo = np.concatenate([weights[:, :HALF], weights[:, HALF + count :]], axis=1)
    return own, halo


def dot(a, b):
    return jnp.dot(a, b, precision=lax.Precision.HIGHEST, preferred_element_type=jnp.float32)


def kernel(
    n_tm, n_tile, levels,
    u_ref, v_ref, land_in, bottom_in, sx_in, sy_in, own_in, halo_in,
    conv_ref, mean_ref,
    land_ref, bottom_ref, sx_ref, sy_ref, own_ref, halo_w_ref, small_sem,
    x, halo, mm, cf, wet, cx, cy, sums, part, edge, edge_halo, edge_mean, edge_in,
    relayed, relay_send, relay_recv,
    x_sem, bulk_send, bulk_recv, edge_send, edge_recv, em_send, em_recv, part_send, part_recv,
):
    snaps, cells, width = u_ref.shape
    rows = cells // levels
    t = lax.axis_index("tm")
    z = lax.axis_index("tile")
    chunks = cells // CHUNK
    fields = (u_ref, v_ref)

    barrier = pltpu.get_barrier_semaphore()
    for k in range(1, n_tm):
        pl.semaphore_signal(barrier, inc=1, device_id={"tm": lax.rem(t + k, n_tm)}, device_id_type=MESH)

    @pl.when(z > 0)
    def _():
        pl.semaphore_signal(barrier, inc=1, device_id={"tile": z - 1}, device_id_type=MESH)

    @pl.when(z < n_tile - 1)
    def _():
        pl.semaphore_signal(barrier, inc=1, device_id={"tile": z + 1}, device_id_type=MESH)

    def local(f, h):
        return pltpu.make_async_copy(
            fields[f].at[:, :, pl.ds(h * LANES, LANES)], x.at[f, h], x_sem.at[f, h]
        )

    small = (
        (land_in, land_ref), (bottom_in, bottom_ref), (sx_in, sx_ref),
        (sy_in, sy_ref), (own_in, own_ref), (halo_in, halo_w_ref),
    )
    for i, (src, dst) in enumerate(small):
        pltpu.make_async_copy(src, dst, small_sem.at[i]).start()
    for f in range(2):
        for h in range(2):
            local(f, h).start()

    pl.semaphore_wait(barrier, n_tm - 1 + (z > 0).astype(jnp.int32) + (z < n_tile - 1).astype(jnp.int32))

    def bulk(side, c, f, h):
        first = snaps - HALF if side == 0 else 0
        to = t + 1 if side == 0 else t - 1
        return pltpu.make_async_remote_copy(
            src_ref=fields[f].at[pl.ds(first, HALF), pl.ds(c * CHUNK, CHUNK), pl.ds(h * LANES, LANES)],
            dst_ref=halo.at[side, f, h, :, pl.ds(c * CHUNK, CHUNK), :],
            send_sem=bulk_send.at[side, c, f, h],
            recv_sem=bulk_recv.at[side, c, f, h],
            device_id={"tm": to},
            device_id_type=MESH,
        )

    middle = (n_tm // 2 - 1, n_tm // 2)
    via = (n_tm - 1, 0)

    def to_relay(side, c, h):
        first = snaps - HALF if side == 0 else 0
        return pltpu.make_async_remote_copy(
            src_ref=fields[1].at[pl.ds(first, HALF), pl.ds(c * CHUNK, CHUNK), pl.ds(h * LANES, LANES)],
            dst_ref=relayed.at[c, h],
            send_sem=bulk_send.at[side, c, 1, h],
            recv_sem=relay_recv.at[c, h],
            device_id={"tm": via[side]},
            device_id_type=MESH,
        )

    def from_relay(side, c, h):
        return pltpu.make_async_remote_copy(
            src_ref=relayed.at[c, h],
            dst_ref=halo.at[side, 1, h, :, pl.ds(c * CHUNK, CHUNK), :],
            send_sem=relay_send.at[c, h],
            recv_sem=bulk_recv.at[side, c, 1, h],
            device_id={"tm": middle[1 - side]},
            device_id_type=MESH,
        )

    def pass_on(c):
        if n_tm < 4:
            return
        for side in range(2):

            @pl.when(t == via[side])
            def _():
                for h in range(2):
                    to_relay(side, c, h).wait_recv()
                    from_relay(side, c, h).start()

    def edge_copy(side):
        first = snaps - HALF if side == 0 else 0
        to = t + 1 if side == 0 else t - 1
        return pltpu.make_async_remote_copy(
            src_ref=edge.at[pl.ds(first, HALF), :],
            dst_ref=edge_halo.at[side],
            send_sem=edge_send.at[side],
            recv_sem=edge_recv.at[side],
            device_id={"tm": to},
            device_id_type=MESH,
        )

    def mean_copy(side):
        to = z + 1 if side == 0 else z - 1
        return pltpu.make_async_remote_copy(
            src_ref=edge_mean,
            dst_ref=edge_in.at[side],
            send_sem=em_send.at[side],
            recv_sem=em_recv.at[side],
            device_id={"tile": to},
            device_id_type=MESH,
        )

    def part_copy(l, k, slot):
        return pltpu.make_async_remote_copy(
            src_ref=part.at[slot, l],
            dst_ref=part.at[slot, l],
            send_sem=part_send.at[l, k],
            recv_sem=part_recv.at[l, k],
            device_id={"tm": lax.rem(t + k, n_tm)},
            device_id_type=MESH,
        )

    sends = (t < n_tm - 1, t > 0)
    receives = (t > 0, t < n_tm - 1)
    z_sends = (z < n_tile - 1, z > 0)
    z_receives = (z > 0, z < n_tile - 1)

    def start_chunk(c):
        for side in range(2):

            if n_tm >= 4:

                @pl.when(t == middle[side])
                def _():
                    for h in range(2):
                        to_relay(side, c, h).start()
                        bulk(side, c, 0, h).start()

                whole = sends[side] & (t != middle[side])
            else:
                whole = sends[side]

            @pl.when(whole)
            def _():
                for f in range(2):
                    for h in range(2):
                        bulk(side, c, f, h).start()

    def finish_chunk(c):
        for side in range(2):

            @pl.when(sends[side])
            def _():
                for f in range(2):
                    for h in range(2):
                        bulk(side, c, f, h).wait_send()

    for c in range(DEPTH):
        start_chunk(c)

    for side in range(2):

        @pl.when(jnp.logical_not(receives[side]))
        def _():
            halo[side] = jnp.zeros(halo.shape[1:], jnp.float32)
            edge_halo[side] = jnp.zeros(edge_halo.shape[1:], jnp.float32)

        @pl.when(jnp.logical_not(z_receives[side]))
        def _():
            edge_in[side] = jnp.zeros(edge_in.shape[1:], jnp.float32)

    for i, (src, dst) in enumerate(small):
        pltpu.make_async_copy(src, dst, small_sem.at[i]).wait()

    for l in range(levels):
        is_wet = (land_ref[...] == 1) & (l < bottom_ref[...])
        level_wet = jnp.where(is_wet, 1.0, 0.0).astype(jnp.float32)
        for j in range(rows):
            wet[l * rows + j] = level_wet[j : j + 1, :]
    all_x, all_y = 0.5 / sx_ref[...], 0.5 / sy_ref[...]
    for j in range(rows):
        cx[j] = all_x[j : j + 1, :]
        cy[j] = all_y[j : j + 1, :]
    for f in range(2):
        for l in range(levels):
            for j in (0, rows + 1):
                mm[f, l, j] = jnp.zeros((snaps, width), jnp.float32)
    column = lax.broadcasted_iota(jnp.int32, (snaps, 2 * HALF), 1)
    valid = ((column >= HALF) | (t > 0)) & ((column < HALF) | (t < n_tm - 1))
    own_w = own_ref[...]
    halo_w = jnp.where(valid, halo_w_ref[...], 0.0)
    weight_sum = jnp.sum(own_w, axis=1, keepdims=True) + jnp.sum(halo_w, axis=1, keepdims=True)
    own_w = own_w / weight_sum
    halo_w = halo_w / weight_sum

    for f in range(2):
        for h in range(2):
            local(f, h).wait()

    def series(ref, count, r):
        return ref.reshape(count * cells, LANES)[pl.ds(r, count, stride=cells), :]

    lane = lax.broadcasted_iota(jnp.int32, (snaps, LANES), 1)

    def pack(r, acc):
        for f in range(2):
            q = f * cells + r
            first = series(x.at[f, 0], snaps, r) * wet[r][:, :LANES]
            acc = jnp.where(lane == q, pltpu.roll(first, q, 1), acc)
            q = (2 + f) * cells + r
            last = series(x.at[f, 1], snaps, r) * wet[r][:, width - LANES :]
            acc = jnp.where(lane == q, pltpu.roll(last, lax.rem(q + 1, LANES), 1), acc)
        return acc

    edge[...] = lax.fori_loop(0, cells, pack, jnp.zeros((snaps, LANES), jnp.float32), unroll=UNROLL)
    for side in range(2):

        @pl.when(sends[side])
        def _():
            edge_copy(side).start()

    pass_on(0)

    def own_part(r, carry):
        l, j = r // rows, lax.rem(r, rows)
        for f in range(2):
            block = jnp.concatenate([series(x.at[f, h], snaps, r) for h in range(2)], axis=1)
            mm[f, l, j + 1] = dot(own_w, block)
        return carry

    lax.fori_loop(0, cells, own_part, 0, unroll=UNROLL)
    for c in range(1, DEPTH):
        pass_on(c)

    for side in range(2):

        @pl.when(receives[side])
        def _():
            edge_copy(side).wait_recv()

    edge_mean[...] = dot(own_w, edge[...]) + dot(
        halo_w, jnp.concatenate([edge_halo[0], edge_halo[1]], axis=0)
    )
    for side in range(2):

        @pl.when(z_sends[side])
        def _():
            mean_copy(side).start()

    wide = lax.broadcasted_iota(jnp.int32, (snaps, width), 1)

    def halo_part(r, carry):
        l, j = r // rows, lax.rem(r, rows)
        mask = wet[r]
        for f in range(2):
            block = jnp.concatenate(
                [
                    jnp.concatenate([series(halo.at[s, f, h], HALF, r) for h in range(2)], axis=1)
                    for s in range(2)
                ],
                axis=0,
            )
            mm[f, l, j + 1] = (mm[f, l, j + 1] + dot(halo_w, block)) * mask
        return carry

    def grad_x(f, r, masked, scale):
        q = (2 + f) * cells + r
        before = pltpu.roll(edge_in[0], lax.rem(2 * LANES - q, LANES), 1)
        q = f * cells + r
        after = pltpu.roll(edge_in[1], lax.rem(2 * LANES - 1 - q, LANES), 1)
        before = jnp.concatenate([before, before], axis=1)
        after = jnp.concatenate([after, after], axis=1)
        behind = jnp.where(wide == 0, before, pltpu.roll(masked, 1, 1))
        ahead = jnp.where(wide == width - 1, after, pltpu.roll(masked, width - 1, 1))
        return (ahead - behind) * scale

    def convert(l):
        def body(j, carry):
            r = l * rows + j
            mask = wet[r]
            scale_x = cx[j]
            scale_y = cy[j]
            eddy, gx, gy = [], [], []
            for f in range(2):
                masked = mm[f, l, j + 1]
                raw = jnp.concatenate([series(x.at[f, h], snaps, r) for h in range(2)], axis=1)
                eddy.append(raw - masked)
                gx.append(grad_x(f, r, masked, scale_x))
                gy.append((mm[f, l, j + 2] - mm[f, l, j]) * scale_y)
            eu, ev = eddy
            total = eu * eu * gx[0] + eu * ev * (gy[0] + gx[1]) + ev * ev * gy[1]
            conversion = -mask * total
            for h in range(2):
                cf.at[h].reshape(snaps * cells, LANES)[pl.ds(r, snaps, stride=cells), :] = conversion[
                    :, h * LANES : (h + 1) * LANES
                ]
            sums[r] = jnp.sum(conversion, axis=0, keepdims=True)
            return carry

        return body

    per_level = rows // CHUNK
    for c in range(chunks):
        finish_chunk(c)
        if c + DEPTH < chunks:
            start_chunk(c + DEPTH)
        for side in range(2):

            @pl.when(receives[side])
            def _():
                for f in range(2):
                    for h in range(2):
                        bulk(side, c, f, h).wait_recv()

        lax.fori_loop(c * CHUNK, (c + 1) * CHUNK, halo_part, 0, unroll=UNROLL)
        if c + DEPTH < chunks:
            pass_on(c + DEPTH)
        if c == 0:
            for side in range(2):

                @pl.when(z_receives[side])
                def _():
                    mean_copy(side).wait_recv()

        l, piece = c // per_level, c % per_level
        low = piece * CHUNK - (1 if piece else 0)
        high = rows if piece == per_level - 1 else (piece + 1) * CHUNK - 1
        lax.fori_loop(low, high, convert(l), 0, unroll=2)
        if piece == per_level - 1:
            part[t, l] = jnp.concatenate([sums[l * rows + j] for j in range(rows)], axis=0)
            for k in range(1, n_tm):
                part_copy(l, k, t).start()

            def narrow(s, carry):
                for h in range(2):
                    conv_ref[s, pl.ds(l * rows, rows), pl.ds(h * LANES, LANES)] = cf[
                        h, s, pl.ds(l * rows, rows), :
                    ].astype(jnp.bfloat16)
                return carry

            lax.fori_loop(0, snaps, narrow, 0)

    for l in range(levels):
        for k in range(1, n_tm):
            part_copy(l, k, lax.rem(t + n_tm - k, n_tm)).wait_recv()
        total = part[0, l]
        for s in range(1, n_tm):
            total = total + part[s, l]
        mean_ref[l] = total / (snaps * n_tm)

    for side in range(2):

        @pl.when(sends[side])
        def _():
            edge_copy(side).wait_send()

        @pl.when(z_sends[side])
        def _():
            mean_copy(side).wait_send()

        if n_tm >= 4:

            @pl.when(t == via[side])
            def _():
                for c in range(chunks):
                    for h in range(2):
                        from_relay(side, c, h).wait_send()

    for l in range(levels):
        for k in range(1, n_tm):
            part_copy(l, k, t).wait_send()


def shards(velocity_u, velocity_v, land_sea, bottom_level, spacing_x, spacing_y):
    snaps, levels, rows, width = velocity_u.shape
    cells = levels * rows
    n_tm, n_tile = lax.axis_size("tm"), lax.axis_size("tile")
    assert width == 2 * LANES and 4 * cells == LANES and snaps >= HALF and rows % CHUNK == 0
    own, halo = band_parts(snaps)
    chunks = cells // CHUNK
    vmem = pl.BlockSpec(memory_space=pltpu.VMEM)
    hbm = pl.BlockSpec(memory_space=pltpu.HBM)
    f32 = jnp.float32
    dma = pltpu.SemaphoreType.DMA
    conversion, mean_map = pl.pallas_call(
        functools.partial(kernel, n_tm, n_tile, levels),
        out_shape=(
            jax.ShapeDtypeStruct((snaps, cells, width), jnp.bfloat16),
            jax.ShapeDtypeStruct((levels, rows, width), f32),
        ),
        in_specs=[hbm] * 8,
        out_specs=(vmem, vmem),
        scratch_shapes=[
            pltpu.VMEM((rows, width), jnp.int32),
            pltpu.VMEM((rows, width), jnp.int32),
            pltpu.VMEM((rows, width), f32),
            pltpu.VMEM((rows, width), f32),
            pltpu.VMEM(own.shape, f32),
            pltpu.VMEM(halo.shape, f32),
            dma((6,)),
            pltpu.VMEM((2, 2, snaps, cells, LANES), f32),
            pltpu.VMEM((2, 2, 2, HALF, cells, LANES), f32),
            pltpu.VMEM((2, levels, rows + 2, snaps, width), f32),
            pltpu.VMEM((2, snaps, cells, LANES), f32),
            pltpu.VMEM((cells, 1, width), f32),
            pltpu.VMEM((rows, 1, width), f32),
            pltpu.VMEM((rows, 1, width), f32),
            pltpu.VMEM((cells, 1, width), f32),
            pltpu.VMEM((n_tm, levels, rows, width), f32),
            pltpu.VMEM((snaps, LANES), f32),
            pltpu.VMEM((2, HALF, LANES), f32),
            pltpu.VMEM((snaps, LANES), f32),
            pltpu.VMEM((2, snaps, LANES), f32),
            pltpu.VMEM((chunks, 2, HALF, CHUNK, LANES), f32),
            dma((chunks, 2)),
            dma((chunks, 2)),
            dma((2, 2)),
            dma((2, chunks, 2, 2)),
            dma((2, chunks, 2, 2)),
            dma((2,)),
            dma((2,)),
            dma((2,)),
            dma((2,)),
            dma((levels, n_tm)),
            dma((levels, n_tm)),
        ],
        compiler_params=pltpu.CompilerParams(
            collective_id=0, has_side_effects=True, vmem_limit_bytes=40 * 1024 * 1024
        ),
        cost_estimate=pl.CostEstimate(flops=10**9, bytes_accessed=4 * 10**6, transcendentals=0),
    )(
        velocity_u.reshape(snaps, cells, width),
        velocity_v.reshape(snaps, cells, width),
        land_sea, bottom_level, spacing_x, spacing_y,
        jnp.asarray(own), jnp.asarray(halo),
    )
    return conversion.reshape(velocity_u.shape), mean_map


def solution(mesh):
    in_specs = (
        P("tm", None, None, "tile"),
        P("tm", None, None, "tile"),
        P(None, "tile"),
        P(None, "tile"),
        P(None, "tile"),
        P(None, "tile"),
    )
    out_specs = (P("tm", None, None, "tile"), P(None, None, "tile"))
    return jax.shard_map(shards, mesh=mesh, in_specs=in_specs, out_specs=out_specs, check_vma=False)
```

profile of v0, /device:TPU:0, one launch (start us, length us, event | category | flops | bytes accessed | tf_op | source)
XLA Modules:
  0.0 50.6 jit_solution(15017090910374728919)
XLA Ops:
  0.6 0.0 copy-start
  0.6 1.4 %copy-done = f32[48,2,16,256]{3,2,1,0:T(8,128)S(1)} copy-done((f32[48,2,16,256]{3,2,1,0:T(8,128)S(1)}, f32[48,2,16,256]{3,2,1,0:T(8,128)}, u32[]{:S(2)}) %copy-start) | copy-done | bytes 1572888
  2.0 0.0 copy-start.1
  2.0 1.4 %copy-done.1 = f32[48,2,16,256]{3,2,1,0:T(8,128)S(1)} copy-done((f32[48,2,16,256]{3,2,1,0:T(8,128)S(1)}, f32[48,2,16,256]{3,2,1,0:T(8,128)}, u32[]{:S(2)}) %copy-start.1) | copy-done | bytes 1572888
  3.4 0.0 copy-start.2
  3.5 0.7 %copy-done.2 = s32[16,256]{1,0:T(8,128)S(1)} copy-done((s32[16,256]{1,0:T(8,128)S(1)}, s32[16,256]{1,0:T(8,128)}, u32[]{:S(2)}) %copy-start.2) | copy-done | bytes 16408
  4.2 0.0 copy-start.3
  4.2 0.7 %copy-done.3 = s32[16,256]{1,0:T(8,128)S(1)} copy-done((s32[16,256]{1,0:T(8,128)S(1)}, s32[16,256]{1,0:T(8,128)}, u32[]{:S(2)}) %copy-start.3) | copy-done | bytes 16408
  4.9 0.0 copy-start.4
  4.9 0.7 %copy-done.4 = f32[16,256]{1,0:T(8,128)S(1)} copy-done((f32[16,256]{1,0:T(8,128)S(1)}, f32[16,256]{1,0:T(8,128)}, u32[]{:S(2)}) %copy-start.4) | copy-done | bytes 16408
  5.6 0.0 copy-start.5
  5.6 0.7 %copy-done.5 = f32[16,256]{1,0:T(8,128)S(1)} copy-done((f32[16,256]{1,0:T(8,128)S(1)}, f32[16,256]{1,0:T(8,128)}, u32[]{:S(2)}) %copy-start.5) | copy-done | bytes 16408
  6.3 0.0 copy-start.6
  6.3 0.7 %copy-done.6 = f32[48,48]{1,0:T(8,128)S(1)} copy-done((f32[48,48]{1,0:T(8,128)S(1)}, f32[48,48]{1,0:T(8,128)}, u32[]{:S(2)}) %copy-start.6) | copy-done | bytes 9240
  7.1 0.0 copy-start.7
  7.1 0.7 %copy-done.7 = f32[48,48]{1,0:T(8,128)S(1)} copy-done((f32[48,48]{1,0:T(8,128)S(1)}, f32[48,48]{1,0:T(8,128)}, u32[]{:S(2)}) %copy-start.7) | copy-done | bytes 9240
  7.8 41.3 %shard_map.95 = (bf16[48,32,256]{2,1,0:T(8,128)(2,1)S(1)}, f32[2,16,256]{2,1,0:T(8,128)S(1)}) custom-call(f32[48,32,256]{2,1,0:T(8,128)S(1)} %bitcast.4, f32[48,32,256]{2,1,0:T(8,128)S(1)} %bitcast.5, s32[16,256]{1,0:T(8,128)S(1)} %copy-done.2, s32[16,256]{1,0:T(8,128)S(1)} %copy-done.3, f32[16,256]{1,0:T(8,128)S(1)} %copy-done.4, f32[16,256]{1,0:T(8,128)S(1)} %copy-done.5, ...), custom_call_target="tpu_custom_call" | custom-call | flops 1000000000 | bytes 4000000 | tf_op jit(solution)/shard_map/pallas_call | solution.py:420
  49.1 0.9 %copy.12 = bf16[48,2,16,256]{3,2,1,0:T(8,128)(2,1)} copy(bf16[48,2,16,256]{3,2,1,0:T(8,128)(2,1)S(1)} %bitcast.3) | data formatting | bytes 1572864
  50.0 0.6 %copy.13 = f32[2,16,256]{2,1,0:T(8,128)} copy(f32[2,16,256]{2,1,0:T(8,128)S(1)} %get-tuple-element.9) | data formatting | bytes 65536
Async XLA Ops:
  0.6 1.4 %copy-start = (f32[48,2,16,256]{3,2,1,0:T(8,128)S(1)}, f32[48,2,16,256]{3,2,1,0:T(8,128)}, u32[]{:S(2)}) copy-start(f32[48,2,16,256]{3,2,1,0:T(8,128)} %param.8) | copy-start | bytes 4718596
  2.0 1.4 %copy-start.1 = (f32[48,2,16,256]{3,2,1,0:T(8,128)S(1)}, f32[48,2,16,256]{3,2,1,0:T(8,128)}, u32[]{:S(2)}) copy-start(f32[48,2,16,256]{3,2,1,0:T(8,128)} %param.9) | copy-start | bytes 4718596
  3.4 0.7 %copy-start.2 = (s32[16,256]{1,0:T(8,128)S(1)}, s32[16,256]{1,0:T(8,128)}, u32[]{:S(2)}) copy-start(s32[16,256]{1,0:T(8,128)} %land_in.1) | copy-start | bytes 49156
  4.2 0.7 %copy-start.3 = (s32[16,256]{1,0:T(8,128)S(1)}, s32[16,256]{1,0:T(8,128)}, u32[]{:S(2)}) copy-start(s32[16,256]{1,0:T(8,128)} %bottom_in.1) | copy-start | bytes 49156
  4.9 0.7 %copy-start.4 = (f32[16,256]{1,0:T(8,128)S(1)}, f32[16,256]{1,0:T(8,128)}, u32[]{:S(2)}) copy-start(f32[16,256]{1,0:T(8,128)} %sx_in.1) | copy-start | bytes 49156
  5.6 0.7 %copy-start.5 = (f32[16,256]{1,0:T(8,128)S(1)}, f32[16,256]{1,0:T(8,128)}, u32[]{:S(2)}) copy-start(f32[16,256]{1,0:T(8,128)} %sy_in.1) | copy-start | bytes 49156
  6.3 0.7 %copy-start.6 = (f32[48,48]{1,0:T(8,128)S(1)}, f32[48,48]{1,0:T(8,128)}, u32[]{:S(2)}) copy-start(f32[48,48]{1,0:T(8,128)} %constant.5.clone.halo_in) | copy-start | bytes 27652
  7.1 0.7 %copy-start.7 = (f32[48,48]{1,0:T(8,128)S(1)}, f32[48,48]{1,0:T(8,128)}, u32[]{:S(2)}) copy-start(f32[48,48]{1,0:T(8,128)} %constant.4.clone.own_in) | copy-start | bytes 27652
where the time goes:
time: 51.1 us; the launch traced here: 50.6 us
  Pallas kernels  41.3 us (81%)
  local copies, waits for them, and re-layouts  8.65 us (17%)
  between operations  0.66 us (1%)
    pallas_call x1, Pallas kernels, shards(): pl.pallas_call(functools.partial(kernel, n_tm, n_tile, levels), out_shape...  41.3 us
    unnamed x18, local copies, waits for them, and re-layouts  8.65 us

commit v1 on v0

--- a/solution.py
+++ b/solution.py
@@ -13,7 +13,6 @@
 LANES = 128
 CHUNK = 8
 DEPTH = 2
-UNROLL = 4
 MESH = pl.DeviceIdType.MESH
 
 
@@ -30,13 +29,33 @@
     return jnp.dot(a, b, precision=lax.Precision.HIGHEST, preferred_element_type=jnp.float32)
 
 
+def halves(a):
+    high = a.astype(jnp.bfloat16).astype(jnp.float32)
+    return high, a - high
+
+
+def stacked_weights(w):
+    high, low = halves(w)
+    return jnp.concatenate(
+        [jnp.concatenate([high, high], axis=1), jnp.concatenate([low, low], axis=1)], axis=0
+    ).astype(jnp.bfloat16)
+
+
+def split_dot(weights, pieces):
+    split = [halves(p) for p in pieces]
+    block = jnp.concatenate([s[0] for s in split] + [s[1] for s in split], axis=0).astype(jnp.bfloat16)
+    both = jnp.dot(weights, block, preferred_element_type=jnp.float32)
+    half = both.shape[0] // 2
+    return both[:half] + both[half:]
+
+
 def kernel(
     n_tm, n_tile, levels,
     u_ref, v_ref, land_in, bottom_in, sx_in, sy_in, own_in, halo_in,
     conv_ref, mean_ref,
     land_ref, bottom_ref, sx_ref, sy_ref, own_ref, halo_w_ref, small_sem,
-    x, halo, mm, cf, wet, cx, cy, sums, part, edge, edge_halo, edge_mean, edge_in,
-    relayed, relay_send, relay_recv,
+    x, halo, mm, cf, wet, cx, cy, part, edge, edge_halo, edge_mean, edge_in,
+    near_w, far_w, relayed, relay_send, relay_recv,
     x_sem, bulk_send, bulk_recv, edge_send, edge_recv, em_send, em_recv, part_send, part_recv,
 ):
     snaps, cells, width = u_ref.shape
@@ -44,7 +63,10 @@
     t = lax.axis_index("tm")
     z = lax.axis_index("tile")
     chunks = cells // CHUNK
+    per_level = rows // CHUNK
     fields = (u_ref, v_ref)
+    even = lax.rem(t, 2) == 0
+    odd = jnp.logical_not(even)
 
     barrier = pltpu.get_barrier_semaphore()
     for k in range(1, n_tm):
@@ -58,9 +80,9 @@
     def _():
         pl.semaphore_signal(barrier, inc=1, device_id={"tile": z + 1}, device_id_type=MESH)
 
-    def local(f, h):
+    def local(c, f, h):
         return pltpu.make_async_copy(
-            fields[f].at[:, :, pl.ds(h * LANES, LANES)], x.at[f, h], x_sem.at[f, h]
+            fields[f].at[:, pl.ds(c * CHUNK, CHUNK), pl.ds(h * LANES, LANES)], x.at[c, f, h], x_sem.at[c, f, h]
         )
 
     small = (
@@ -69,18 +91,17 @@
     )
     for i, (src, dst) in enumerate(small):
         pltpu.make_async_copy(src, dst, small_sem.at[i]).start()
-    for f in range(2):
-        for h in range(2):
-            local(f, h).start()
-
-    pl.semaphore_wait(barrier, n_tm - 1 + (z > 0).astype(jnp.int32) + (z < n_tile - 1).astype(jnp.int32))
+    for c in range(chunks):
+        for f in range(2):
+            for h in range(2):
+                local(c, f, h).start()
 
     def bulk(side, c, f, h):
         first = snaps - HALF if side == 0 else 0
         to = t + 1 if side == 0 else t - 1
         return pltpu.make_async_remote_copy(
             src_ref=fields[f].at[pl.ds(first, HALF), pl.ds(c * CHUNK, CHUNK), pl.ds(h * LANES, LANES)],
-            dst_ref=halo.at[side, f, h, :, pl.ds(c * CHUNK, CHUNK), :],
+            dst_ref=halo.at[side, c, f, h],
             send_sem=bulk_send.at[side, c, f, h],
             recv_sem=bulk_recv.at[side, c, f, h],
             device_id={"tm": to},
@@ -104,7 +125,7 @@
     def from_relay(side, c, h):
         return pltpu.make_async_remote_copy(
             src_ref=relayed.at[c, h],
-            dst_ref=halo.at[side, 1, h, :, pl.ds(c * CHUNK, CHUNK), :],
+            dst_ref=halo.at[side, c, 1, h],
             send_sem=relay_send.at[c, h],
             recv_sem=bulk_recv.at[side, c, 1, h],
             device_id={"tm": middle[1 - side]},
@@ -145,24 +166,32 @@
             device_id_type=MESH,
         )
 
-    def part_copy(l, k, slot):
+    def converted(c):
+        piece = c % per_level
+        low = piece * CHUNK - (1 if piece else 0)
+        high = rows if piece == per_level - 1 else (piece + 1) * CHUNK - 1
+        return c // per_level, low, high
+
+    def part_copy(c, k, slot):
+        l, low, high = converted(c)
         return pltpu.make_async_remote_copy(
-            src_ref=part.at[slot, l],
-            dst_ref=part.at[slot, l],
-            send_sem=part_send.at[l, k],
-            recv_sem=part_recv.at[l, k],
+            src_ref=part.at[slot, pl.ds(l * rows + low, high - low)],
+            dst_ref=part.at[slot, pl.ds(l * rows + low, high - low)],
+            send_sem=part_send.at[c, k],
+            recv_sem=part_recv.at[c, k],
             device_id={"tm": lax.rem(t + k, n_tm)},
             device_id_type=MESH,
         )
 
     sends = (t < n_tm - 1, t > 0)
     receives = (t > 0, t < n_tm - 1)
+    send_near, send_far = (even, odd), (odd, even)
+    near, far = (odd, even), (even, odd)
     z_sends = (z < n_tile - 1, z > 0)
     z_receives = (z > 0, z < n_tile - 1)
 
-    def start_chunk(c):
+    def start_far(c):
         for side in range(2):
-
             if n_tm >= 4:
 
                 @pl.when(t == middle[side])
@@ -171,9 +200,9 @@
                         to_relay(side, c, h).start()
                         bulk(side, c, 0, h).start()
 
-                whole = sends[side] & (t != middle[side])
+                whole = sends[side] & send_far[side] & (t != middle[side])
             else:
-                whole = sends[side]
+                whole = sends[side] & send_far[side]
 
             @pl.when(whole)
             def _():
@@ -181,17 +210,27 @@
                     for h in range(2):
                         bulk(side, c, f, h).start()
 
-    def finish_chunk(c):
+    def finish_send(c, which):
         for side in range(2):
 
-            @pl.when(sends[side])
+            @pl.when(sends[side] & which[side])
             def _():
                 for f in range(2):
                     for h in range(2):
                         bulk(side, c, f, h).wait_send()
 
+    pl.semaphore_wait(barrier, n_tm - 1 + (z > 0).astype(jnp.int32) + (z < n_tile - 1).astype(jnp.int32))
+
     for c in range(DEPTH):
-        start_chunk(c)
+        start_far(c)
+    for side in range(2):
+
+        @pl.when(sends[side] & send_near[side])
+        def _():
+            for c in range(chunks):
+                for f in range(2):
+                    for h in range(2):
+                        bulk(side, c, f, h).start()
 
     for side in range(2):
 
@@ -227,27 +266,38 @@
     weight_sum = jnp.sum(own_w, axis=1, keepdims=True) + jnp.sum(halo_w, axis=1, keepdims=True)
     own_w = own_w / weight_sum
     halo_w = halo_w / weight_sum
-
-    for f in range(2):
-        for h in range(2):
-            local(f, h).wait()
-
-    def series(ref, count, r):
-        return ref.reshape(count * cells, LANES)[pl.ds(r, count, stride=cells), :]
+    near_side = 1 - lax.rem(t, 2)
+    far_side = lax.rem(t, 2)
+    near_half = jnp.where(even, halo_w[:, HALF:], halo_w[:, :HALF])
+    far_half = jnp.where(even, halo_w[:, :HALF], halo_w[:, HALF:])
+    near_w[...] = stacked_weights(jnp.concatenate([own_w, near_half], axis=1))
+    far_w[...] = stacked_weights(far_half)
+
+    for c in range(chunks):
+        for f in range(2):
+            for h in range(2):
+                local(c, f, h).wait()
+
+    def series(ref, count, j):
+        return ref.reshape(count * CHUNK, LANES)[pl.ds(j, count, stride=CHUNK), :]
+
+    def both(ref, count, j):
+        return jnp.concatenate([series(ref.at[h], count, j) for h in range(2)], axis=1)
 
     lane = lax.broadcasted_iota(jnp.int32, (snaps, LANES), 1)
 
     def pack(r, acc):
+        c, j = r // CHUNK, lax.rem(r, CHUNK)
         for f in range(2):
             q = f * cells + r
-            first = series(x.at[f, 0], snaps, r) * wet[r][:, :LANES]
+            first = series(x.at[c, f, 0], snaps, j) * wet[r][:, :LANES]
             acc = jnp.where(lane == q, pltpu.roll(first, q, 1), acc)
             q = (2 + f) * cells + r
-            last = series(x.at[f, 1], snaps, r) * wet[r][:, width - LANES :]
+            last = series(x.at[c, f, 1], snaps, j) * wet[r][:, width - LANES :]
             acc = jnp.where(lane == q, pltpu.roll(last, lax.rem(q + 1, LANES), 1), acc)
         return acc
 
-    edge[...] = lax.fori_loop(0, cells, pack, jnp.zeros((snaps, LANES), jnp.float32), unroll=UNROLL)
+    edge[...] = lax.fori_loop(0, cells, pack, jnp.zeros((snaps, LANES), jnp.float32), unroll=4)
     for side in range(2):
 
         @pl.when(sends[side])
@@ -256,14 +306,24 @@
 
     pass_on(0)
 
-    def own_part(r, carry):
+    for side in range(2):
+
+        @pl.when(receives[side] & near[side])
+        def _():
+            for c in range(chunks):
+                for f in range(2):
+                    for h in range(2):
+                        bulk(side, c, f, h).wait_recv()
+
+    def near_part(r, carry):
         l, j = r // rows, lax.rem(r, rows)
+        c, i = r // CHUNK, lax.rem(r, CHUNK)
         for f in range(2):
-            block = jnp.concatenate([series(x.at[f, h], snaps, r) for h in range(2)], axis=1)
-            mm[f, l, j + 1] = dot(own_w, block)
+            pieces = [both(x.at[c, f], snaps, i), both(halo.at[near_side, c, f], HALF, i)]
+            mm[f, l, j + 1] = split_dot(near_w[...], pieces)
         return carry
 
-    lax.fori_loop(0, cells, own_part, 0, unroll=UNROLL)
+    lax.fori_loop(0, cells, near_part, 0, unroll=8)
     for c in range(1, DEPTH):
         pass_on(c)
 
@@ -284,18 +344,13 @@
 
     wide = lax.broadcasted_iota(jnp.int32, (snaps, width), 1)
 
-    def halo_part(r, carry):
+    def far_part(r, carry):
         l, j = r // rows, lax.rem(r, rows)
+        c, i = r // CHUNK, lax.rem(r, CHUNK)
         mask = wet[r]
         for f in range(2):
-            block = jnp.concatenate(
-                [
-                    jnp.concatenate([series(halo.at[s, f, h], HALF, r) for h in range(2)], axis=1)
-                    for s in range(2)
-                ],
-                axis=0,
-            )
-            mm[f, l, j + 1] = (mm[f, l, j + 1] + dot(halo_w, block)) * mask
+            pieces = [both(halo.at[far_side, c, f], HALF, i)]
+            mm[f, l, j + 1] = (mm[f, l, j + 1] + split_dot(far_w[...], pieces)) * mask
         return carry
 
     def grad_x(f, r, masked, scale):
@@ -312,42 +367,41 @@
     def convert(l):
         def body(j, carry):
             r = l * rows + j
+            c, i = r // CHUNK, lax.rem(r, CHUNK)
             mask = wet[r]
             scale_x = cx[j]
             scale_y = cy[j]
             eddy, gx, gy = [], [], []
             for f in range(2):
                 masked = mm[f, l, j + 1]
-                raw = jnp.concatenate([series(x.at[f, h], snaps, r) for h in range(2)], axis=1)
-                eddy.append(raw - masked)
+                eddy.append(both(x.at[c, f], snaps, i) - masked)
                 gx.append(grad_x(f, r, masked, scale_x))
                 gy.append((mm[f, l, j + 2] - mm[f, l, j]) * scale_y)
             eu, ev = eddy
             total = eu * eu * gx[0] + eu * ev * (gy[0] + gx[1]) + ev * ev * gy[1]
             conversion = -mask * total
             for h in range(2):
-                cf.at[h].reshape(snaps * cells, LANES)[pl.ds(r, snaps, stride=cells), :] = conversion[
+                cf.at[c, h].reshape(snaps * CHUNK, LANES)[pl.ds(i, snaps, stride=CHUNK), :] = conversion[
                     :, h * LANES : (h + 1) * LANES
                 ]
-            sums[r] = jnp.sum(conversion, axis=0, keepdims=True)
+            part[t, r] = jnp.sum(conversion, axis=0, keepdims=True)
             return carry
 
         return body
 
-    per_level = rows // CHUNK
     for c in range(chunks):
-        finish_chunk(c)
+        finish_send(c, send_far)
         if c + DEPTH < chunks:
-            start_chunk(c + DEPTH)
+            start_far(c + DEPTH)
         for side in range(2):
 
-            @pl.when(receives[side])
+            @pl.when(receives[side] & far[side])
             def _():
                 for f in range(2):
                     for h in range(2):
                         bulk(side, c, f, h).wait_recv()
 
-        lax.fori_loop(c * CHUNK, (c + 1) * CHUNK, halo_part, 0, unroll=UNROLL)
+        lax.fori_loop(c * CHUNK, (c + 1) * CHUNK, far_part, 0, unroll=8)
         if c + DEPTH < chunks:
             pass_on(c + DEPTH)
         if c == 0:
@@ -357,32 +411,32 @@
                 def _():
                     mean_copy(side).wait_recv()
 
-        l, piece = c // per_level, c % per_level
-        low = piece * CHUNK - (1 if piece else 0)
-        high = rows if piece == per_level - 1 else (piece + 1) * CHUNK - 1
+        l, low, high = converted(c)
         lax.fori_loop(low, high, convert(l), 0, unroll=2)
-        if piece == per_level - 1:
-            part[t, l] = jnp.concatenate([sums[l * rows + j] for j in range(rows)], axis=0)
-            for k in range(1, n_tm):
-                part_copy(l, k, t).start()
+        for k in range(1, n_tm):
+            part_copy(c, k, t).start()
+        if c % per_level == per_level - 1:
 
             def narrow(s, carry):
                 for h in range(2):
-                    conv_ref[s, pl.ds(l * rows, rows), pl.ds(h * LANES, LANES)] = cf[
-                        h, s, pl.ds(l * rows, rows), :
-                    ].astype(jnp.bfloat16)
+                    block = jnp.concatenate([cf[l * per_level + p, h, s] for p in range(per_level)], axis=0)
+                    conv_ref[s, pl.ds(l * rows, rows), pl.ds(h * LANES, LANES)] = block.astype(jnp.bfloat16)
                 return carry
 
-            lax.fori_loop(0, snaps, narrow, 0)
-
-    for l in range(levels):
+            lax.fori_loop(0, snaps, narrow, 0, unroll=4)
+
+    for c in range(chunks):
         for k in range(1, n_tm):
-            part_copy(l, k, lax.rem(t + n_tm - k, n_tm)).wait_recv()
-        total = part[0, l]
-        for s in range(1, n_tm):
-            total = total + part[s, l]
-        mean_ref[l] = total / (snaps * n_tm)
-
+            part_copy(c, k, lax.rem(t + n_tm - k, n_tm)).wait_recv()
+        l, low, high = converted(c)
+        for j in range(low, high):
+            total = part[0, l * rows + j]
+            for s in range(1, n_tm):
+                total = total + part[s, l * rows + j]
+            mean_ref[l, j : j + 1, :] = total / (snaps * n_tm)
+
+    for c in range(chunks):
+        finish_send(c, send_near)
     for side in range(2):
 
         @pl.when(sends[side])
@@ -401,26 +455,26 @@
                     for h in range(2):
                         from_relay(side, c, h).wait_send()
 
-    for l in range(levels):
+    for c in range(chunks):
         for k in range(1, n_tm):
-            part_copy(l, k, t).wait_send()
+            part_copy(c, k, t).wait_send()
 
 
 def shards(velocity_u, velocity_v, land_sea, bottom_level, spacing_x, spacing_y):
     snaps, levels, rows, width = velocity_u.shape
     cells = levels * rows
     n_tm, n_tile = lax.axis_size("tm"), lax.axis_size("tile")
-    assert width == 2 * LANES and 4 * cells == LANES and snaps >= HALF and rows % CHUNK == 0
+    assert width == 2 * LANES and 4 * cells == LANES and snaps >= HALF and rows % CHUNK == 0 and n_tm % 4 == 0
     own, halo = band_parts(snaps)
     chunks = cells // CHUNK
     vmem = pl.BlockSpec(memory_space=pltpu.VMEM)
     hbm = pl.BlockSpec(memory_space=pltpu.HBM)
-    f32 = jnp.float32
+    f32, bf16 = jnp.float32, jnp.bfloat16
     dma = pltpu.SemaphoreType.DMA
     conversion, mean_map = pl.pallas_call(
         functools.partial(kernel, n_tm, n_tile, levels),
         out_shape=(
-            jax.ShapeDtypeStruct((snaps, cells, width), jnp.bfloat16),
+            jax.ShapeDtypeStruct((snaps, cells, width), bf16),
             jax.ShapeDtypeStruct((levels, rows, width), f32),
         ),
         in_specs=[hbm] * 8,
@@ -433,34 +487,35 @@
             pltpu.VMEM(own.shape, f32),
             pltpu.VMEM(halo.shape, f32),
             dma((6,)),
-            pltpu.VMEM((2, 2, snaps, cells, LANES), f32),
-            pltpu.VMEM((2, 2, 2, HALF, cells, LANES), f32),
+            pltpu.VMEM((chunks, 2, 2, snaps, CHUNK, LANES), f32),
+            pltpu.VMEM((2, chunks, 2, 2, HALF, CHUNK, LANES), f32),
             pltpu.VMEM((2, levels, rows + 2, snaps, width), f32),
-            pltpu.VMEM((2, snaps, cells, LANES), f32),
+            pltpu.VMEM((chunks, 2, snaps, CHUNK, LANES), f32),
             pltpu.VMEM((cells, 1, width), f32),
             pltpu.VMEM((rows, 1, width), f32),
             pltpu.VMEM((rows, 1, width), f32),
-            pltpu.VMEM((cells, 1, width), f32),
-            pltpu.VMEM((n_tm, levels, rows, width), f32),
+            pltpu.VMEM((n_tm, cells, 1, width), f32),
             pltpu.VMEM((snaps, LANES), f32),
             pltpu.VMEM((2, HALF, LANES), f32),
             pltpu.VMEM((snaps, LANES), f32),
             pltpu.VMEM((2, snaps, LANES), f32),
+            pltpu.VMEM((2 * snaps, 2 * (snaps + HALF)), bf16),
+            pltpu.VMEM((2 * snaps, 2 * HALF), bf16),
             pltpu.VMEM((chunks, 2, HALF, CHUNK, LANES), f32),
             dma((chunks, 2)),
             dma((chunks, 2)),
-            dma((2, 2)),
+            dma((chunks, 2, 2)),
             dma((2, chunks, 2, 2)),
             dma((2, chunks, 2, 2)),
             dma((2,)),
             dma((2,)),
             dma((2,)),
             dma((2,)),
-            dma((levels, n_tm)),
-            dma((levels, n_tm)),
+            dma((chunks, n_tm)),
+            dma((chunks, n_tm)),
         ],
         compiler_params=pltpu.CompilerParams(
-            collective_id=0, has_side_effects=True, vmem_limit_bytes=40 * 1024 * 1024
+            collective_id=0, has_side_effects=True, vmem_limit_bytes=60 * 1024 * 1024
         ),
         cost_estimate=pl.CostEstimate(flops=10**9, bytes_accessed=4 * 10**6, transcendentals=0),
     )(

time: 51.1 us -> 45.6 us (0.89)
  local copies, waits for them, and re-layouts: 8.65 us -> 2.69 us
  Pallas kernels: 41.3 us -> 42.2 us
    unnamed x18 -> x4, local copies, waits for them, and re-layouts: 8.65 us -> 2.69 us
    pallas_call x1, Pallas kernels: 41.3 us -> 42.2 us  [shards(): pl.pallas_call(functools.partial(kernel, n_tm, n_tile, levels), out_shape...]
where the time goes in v1:
time: 45.6 us; the launch traced here: 45.5 us
  Pallas kernels  42.2 us (93%)
  local copies, waits for them, and re-layouts  2.69 us (6%)
  between operations  0.65 us (1%)
    pallas_call x1, Pallas kernels, shards(): pl.pallas_call(functools.partial(kernel, n_tm, n_tile, levels), out_shape...  42.2 us
    unnamed x4, local copies, waits for them, and re-layouts  2.69 us

profile of v1, /device:TPU:0, one launch (start us, length us, event | category | flops | bytes accessed | tf_op | source)
XLA Modules:
  0.0 45.5 jit_solution(9376468846571226888)
XLA Ops:
  0.6 42.2 %shard_map.95 = (bf16[48,32,256]{2,1,0:T(8,128)(2,1)}, f32[2,16,256]{2,1,0:T(8,128)}) custom-call(f32[48,32,256]{2,1,0:T(8,128)} %bitcast.4, f32[48,32,256]{2,1,0:T(8,128)} %bitcast.5, s32[16,256]{1,0:T(8,128)} %land_in.1, s32[16,256]{1,0:T(8,128)} %bottom_in.1, f32[16,256]{1,0:T(8,128)} %sx_in.1, f32[16,256]{1,0:T(8,128)} %sy_in.1, ...), custom_call_target="tpu_custom_call" | custom-call | flops 1000000000 | bytes 4000000 | tf_op jit(solution)/shard_map/pallas_call | solution.py:474
  42.8 0.0 copy-start
  42.8 2.1 %copy.12 = bf16[48,2,16,256]{3,2,1,0:T(8,128)(2,1)} copy(bf16[48,2,16,256]{3,2,1,0:T(8,128)(2,1)} %bitcast.3) | data formatting | bytes 1572864
  44.9 0.0 copy-done
  44.9 0.6 %copy.13 = f32[2,16,256]{2,1,0:T(8,128)} copy(f32[2,16,256]{2,1,0:T(8,128)S(1)} %copy-done) | data formatting | bytes 65536
Async XLA Ops:
  42.8 2.1 %copy-start = (f32[2,16,256]{2,1,0:T(8,128)S(1)}, f32[2,16,256]{2,1,0:T(8,128)}, u32[]{:S(2)}) copy-start(f32[2,16,256]{2,1,0:T(8,128)} %get-tuple-element.9) | copy-start | bytes 98308

commit v2 on v1

--- a/solution.py
+++ b/solution.py
@@ -460,18 +460,527 @@
             part_copy(c, k, t).wait_send()
 
 
-def shards(velocity_u, velocity_v, land_sea, bottom_level, spacing_x, spacing_y):
-    snaps, levels, rows, width = velocity_u.shape
-    cells = levels * rows
+def fast_kernel(
+    n_tm, n_tile, levels,
+    u_ref, v_ref, land_in, bottom_in, sx_in, sy_in, own_in, halo_in,
+    conv_ref, mean_ref, flag_ref,
+    land_ref, bottom_ref, sx_ref, sy_ref, own_ref, halo_w_ref, small_sem,
+    x, near, mm, cf, wet, key, cx, cy, part, edge, edge_halo, edge_mean, edge_in,
+    near_w, far_w, place, packed, far, relayed, flags,
+    relay_send, relay_recv, x_sem, near_sem, far_send, far_recv, edge_send, edge_recv, em_send, em_recv,
+    part_send, part_recv, flag_send, flag_recv,
+):
+    snaps, cells, width = u_ref.shape
+    rows = cells // levels
+    t = lax.axis_index("tm")
+    z = lax.axis_index("tile")
+    chunks = cells // CHUNK
+    per_level = rows // CHUNK
+    fields = (u_ref, v_ref)
+    even = lax.rem(t, 2) == 0
+    odd = jnp.logical_not(even)
+
+    barrier = pltpu.get_barrier_semaphore()
+    for k in range(1, n_tm):
+        pl.semaphore_signal(barrier, inc=1, device_id={"tm": lax.rem(t + k, n_tm)}, device_id_type=MESH)
+    for k in range(1, n_tile):
+        pl.semaphore_signal(barrier, inc=1, device_id={"tile": lax.rem(z + k, n_tile)}, device_id_type=MESH)
+
+    def local(c, f, h):
+        return pltpu.make_async_copy(
+            fields[f].at[:, pl.ds(c * CHUNK, CHUNK), pl.ds(h * LANES, LANES)], x.at[c, f, h], x_sem.at[c, f, h]
+        )
+
+    small = (
+        (land_in, land_ref), (bottom_in, bottom_ref), (sx_in, sx_ref),
+        (sy_in, sy_ref), (own_in, own_ref), (halo_in, halo_w_ref),
+    )
+    for i, (src, dst) in enumerate(small):
+        pltpu.make_async_copy(src, dst, small_sem.at[i]).start()
+    for c in range(chunks):
+        for f in range(2):
+            for h in range(2):
+                local(c, f, h).start()
+
+    first_far = jnp.where(even, 0, snaps - HALF)
+    first_near = jnp.where(even, snaps - HALF, 0)
+    has_far = (t > 0) & (t < n_tm - 1)
+    at_end = jnp.logical_not(has_far)
+    is_middle = (t == n_tm // 2 - 1) | (t == n_tm // 2)
+    far_to = jnp.where(even, t - 1, t + 1)
+    via_to = jnp.where(t < n_tm // 2, n_tm - 1, 0)
+    forward_to = jnp.where(t == 0, n_tm // 2 - 1, n_tm // 2)
+
+    def tiles(c):
+        wide = CHUNK * 3 // 2
+        l = c // per_level
+        start = c * wide if l == 0 else per_level * wide + (c - per_level) * CHUNK
+        return start, wide if l == 0 else CHUNK
+
+    def near_copy():
+        return pltpu.make_async_remote_copy(
+            src_ref=x.at[:, :, :, pl.ds(first_near, HALF)],
+            dst_ref=near,
+            send_sem=near_sem.at[0],
+            recv_sem=near_sem.at[1],
+            device_id={"tm": t + 1 - 2 * lax.rem(t, 2)},
+            device_id_type=MESH,
+        )
+
+    def far_copy(c, f):
+        start, count = tiles(c)
+        return pltpu.make_async_remote_copy(
+            src_ref=packed.at[f, pl.ds(start, count)],
+            dst_ref=far.at[f, pl.ds(start, count)],
+            send_sem=far_send.at[c, f],
+            recv_sem=far_recv.at[c, f],
+            device_id={"tm": far_to},
+            device_id_type=MESH,
+        )
+
+    def to_relay(c):
+        start, count = tiles(c)
+        return pltpu.make_async_remote_copy(
+            src_ref=packed.at[1, pl.ds(start, count)],
+            dst_ref=relayed.at[pl.ds(start, count)],
+            send_sem=far_send.at[c, 1],
+            recv_sem=relay_recv.at[c],
+            device_id={"tm": via_to},
+            device_id_type=MESH,
+        )
+
+    def from_relay(c):
+        start, count = tiles(c)
+        return pltpu.make_async_remote_copy(
+            src_ref=relayed.at[pl.ds(start, count)],
+            dst_ref=far.at[1, pl.ds(start, count)],
+            send_sem=relay_send.at[c],
+            recv_sem=far_recv.at[c, 1],
+            device_id={"tm": forward_to},
+            device_id_type=MESH,
+        )
+
+    def pass_on(c):
+        @pl.when(at_end)
+        def _():
+            to_relay(c).wait_recv()
+            from_relay(c).start()
+
+    def start_far(c):
+        @pl.when(has_far)
+        def _():
+            far_copy(c, 0).start()
+
+        @pl.when(is_middle)
+        def _():
+            to_relay(c).start()
+
+        @pl.when(has_far & jnp.logical_not(is_middle))
+        def _():
+            far_copy(c, 1).start()
+
+    def edge_copy(side):
+        first = snaps - HALF if side == 0 else 0
+        to = t + 1 if side == 0 else t - 1
+        return pltpu.make_async_remote_copy(
+            src_ref=edge.at[pl.ds(first, HALF), :],
+            dst_ref=edge_halo.at[side],
+            send_sem=edge_send.at[side],
+            recv_sem=edge_recv.at[side],
+            device_id={"tm": to},
+            device_id_type=MESH,
+        )
+
+    def mean_copy(side):
+        to = z + 1 if side == 0 else z - 1
+        return pltpu.make_async_remote_copy(
+            src_ref=edge_mean,
+            dst_ref=edge_in.at[side],
+            send_sem=em_send.at[side],
+            recv_sem=em_recv.at[side],
+            device_id={"tile": to},
+            device_id_type=MESH,
+        )
+
+    def flag_copy(k, slot):
+        return pltpu.make_async_remote_copy(
+            src_ref=flags.at[slot],
+            dst_ref=flags.at[slot],
+            send_sem=flag_send.at[k],
+            recv_sem=flag_recv.at[k],
+            device_id={"tile": lax.rem(z + k, n_tile)},
+            device_id_type=MESH,
+        )
+
+    def converted(c):
+        piece = c % per_level
+        low = piece * CHUNK - (1 if piece else 0)
+        high = rows if piece == per_level - 1 else (piece + 1) * CHUNK - 1
+        return c // per_level, low, high
+
+    def part_copy(c, k, slot):
+        l, low, high = converted(c)
+        return pltpu.make_async_remote_copy(
+            src_ref=part.at[slot, pl.ds(l * rows + low, high - low)],
+            dst_ref=part.at[slot, pl.ds(l * rows + low, high - low)],
+            send_sem=part_send.at[c, k],
+            recv_sem=part_recv.at[c, k],
+            device_id={"tm": lax.rem(t + k, n_tm)},
+            device_id_type=MESH,
+        )
+
+    sends = (t < n_tm - 1, t > 0)
+    receives = (t > 0, t < n_tm - 1)
+    z_sends = (z < n_tile - 1, z > 0)
+    z_receives = (z > 0, z < n_tile - 1)
+
+    for i, (src, dst) in enumerate(small):
+        pltpu.make_async_copy(src, dst, small_sem.at[i]).wait()
+
+    levels_wet = []
+    for l in range(levels):
+        is_wet = (land_ref[...] == 1) & (l < bottom_ref[...])
+        levels_wet.append(jnp.where(is_wet, 1.0, 0.0).astype(jnp.float32))
+    all_wet = jnp.concatenate(levels_wet, axis=0)
+    lower = lax.broadcasted_iota(jnp.int32, (width, width), 0)
+    upper = lax.broadcasted_iota(jnp.int32, (width, width), 1)
+    before = jnp.where(lower < upper, 1.0, 0.0).astype(jnp.bfloat16)
+    order = jnp.dot(all_wet.astype(jnp.bfloat16), before, preferred_element_type=jnp.float32)
+    row = lax.broadcasted_iota(jnp.int32, (cells, width), 0)
+    room = jnp.where(row < rows, float(width * 3 // 4), float(width // 2))
+    shift = jnp.where((row < rows) & (lax.rem(row, 2) == 1), float(width // 4), 0.0)
+    all_key = jnp.where((all_wet > 0.0) & (order < room), order + shift, -1.0)
+    over = jnp.max(order + all_wet - room, axis=0, keepdims=True)
+    flags[z] = jnp.broadcast_to(jnp.maximum(over[:, :LANES], over[:, LANES:]), (8, LANES))
+    for r in range(cells):
+        wet[r] = all_wet[r : r + 1, :]
+        key[r] = all_key[r : r + 1, :]
+
+    def series(ref, count, j):
+        return ref.reshape(count * CHUNK, LANES)[pl.ds(j, count, stride=CHUNK), :]
+
+    def both(ref, count, j):
+        return jnp.concatenate([series(ref.at[h], count, j) for h in range(2)], axis=1)
+
+    def put(size):
+        index = lax.broadcasted_iota(jnp.int32, (size, width), 0).astype(jnp.float32)
+
+        def body(r, carry):
+            place[r, :size] = jnp.where(index == key[r], 1.0, 0.0).astype(jnp.bfloat16)
+            return carry
+
+        return body
+
+    def gather(c, i, size):
+        split = []
+        for f in range(2):
+            block = [x.at[c, f, h].reshape(snaps * CHUNK, LANES) for h in range(2)]
+            at = pl.ds(first_far * CHUNK + i, HALF, stride=CHUNK)
+            split.extend(halves(jnp.concatenate([b[at, :] for b in block], axis=1)))
+        split = jnp.concatenate(split, axis=0).astype(jnp.bfloat16)
+        out = lax.dot_general(
+            split, place[c * CHUNK + i, :size], (((1,), (1,)), ((), ())), preferred_element_type=jnp.float32
+        )
+        return [out[2 * f * HALF : (2 * f + 1) * HALF] + out[(2 * f + 1) * HALF : (2 * f + 2) * HALF] for f in range(2)]
+
+    def compact(c):
+        start, _ = tiles(c)
+        if c < per_level:
+            lax.fori_loop(c * CHUNK, (c + 1) * CHUNK, put(width), 0, unroll=2)
+
+            def body(m, carry):
+                one, two = gather(c, 2 * m, width), gather(c, 2 * m + 1, width)
+                for f in range(2):
+                    packed[f, start + 3 * m] = one[f][:, :LANES]
+                    packed[f, start + 3 * m + 1] = one[f][:, LANES:] + two[f][:, :LANES]
+                    packed[f, start + 3 * m + 2] = two[f][:, LANES:]
+                return carry
+
+            lax.fori_loop(0, CHUNK // 2, body, 0, unroll=2)
+        else:
+            lax.fori_loop(c * CHUNK, (c + 1) * CHUNK, put(LANES), 0, unroll=4)
+
+            def body(i, carry):
+                one = gather(c, i, LANES)
+                for f in range(2):
+                    packed[f, start + i] = one[f]
+                return carry
+
+            lax.fori_loop(0, CHUNK, body, 0, unroll=4)
+
+    def wait_local(c):
+        for f in range(2):
+            for h in range(2):
+                local(c, f, h).wait()
+
+    wait_local(0)
+    compact(0)
+    pl.semaphore_wait(barrier, n_tm - 1 + n_tile - 1)
+    start_far(0)
+    for k in range(1, n_tile):
+        flag_copy(k, z).start()
+    for c in range(1, chunks):
+        wait_local(c)
+    near_copy().start()
+    compact(1)
+    if DEPTH > 1:
+        start_far(1)
+
+    @pl.when(at_end)
+    def _():
+        far[...] = jnp.zeros(far.shape, jnp.float32)
+
+    for side in range(2):
+
+        @pl.when(jnp.logical_not(receives[side]))
+        def _():
+            edge_halo[side] = jnp.zeros(edge_halo.shape[1:], jnp.float32)
+
+        @pl.when(jnp.logical_not(z_receives[side]))
+        def _():
+            edge_in[side] = jnp.zeros(edge_in.shape[1:], jnp.float32)
+
+    all_x, all_y = 0.5 / sx_ref[...], 0.5 / sy_ref[...]
+    for j in range(rows):
+        cx[j] = all_x[j : j + 1, :]
+        cy[j] = all_y[j : j + 1, :]
+    for f in range(2):
+        for l in range(levels):
+            for j in (0, rows + 1):
+                mm[f, l, j] = jnp.zeros((snaps, width), jnp.float32)
+    column = lax.broadcasted_iota(jnp.int32, (snaps, 2 * HALF), 1)
+    valid = ((column >= HALF) | (t > 0)) & ((column < HALF) | (t < n_tm - 1))
+    own_w = own_ref[...]
+    halo_w = jnp.where(valid, halo_w_ref[...], 0.0)
+    weight_sum = jnp.sum(own_w, axis=1, keepdims=True) + jnp.sum(halo_w, axis=1, keepdims=True)
+    own_w = own_w / weight_sum
+    halo_w = halo_w / weight_sum
+    near_half = jnp.where(even, halo_w[:, HALF:], halo_w[:, :HALF])
+    far_half = jnp.where(even, halo_w[:, :HALF], halo_w[:, HALF:])
+    near_w[...] = stacked_weights(jnp.concatenate([own_w, near_half], axis=1))
+    far_w[...] = stacked_weights(far_half)
+
+    lane = lax.broadcasted_iota(jnp.int32, (snaps, LANES), 1)
+
+    def pack(r, acc):
+        c, j = r // CHUNK, lax.rem(r, CHUNK)
+        for f in range(2):
+            q = f * cells + r
+            first = series(x.at[c, f, 0], snaps, j) * wet[r][:, :LANES]
+            acc = jnp.where(lane == q, pltpu.roll(first, q, 1), acc)
+            q = (2 + f) * cells + r
+            last = series(x.at[c, f, 1], snaps, j) * wet[r][:, width - LANES :]
+            acc = jnp.where(lane == q, pltpu.roll(last, lax.rem(q + 1, LANES), 1), acc)
+        return acc
+
+    edge[...] = lax.fori_loop(0, cells, pack, jnp.zeros((snaps, LANES), jnp.float32), unroll=4)
+    for side in range(2):
+
+        @pl.when(sends[side])
+        def _():
+            edge_copy(side).start()
+
+    pass_on(0)
+    near_copy().wait_recv()
+
+    def near_part(r, carry):
+        l, j = r // rows, lax.rem(r, rows)
+        c, i = r // CHUNK, lax.rem(r, CHUNK)
+        for f in range(2):
+            pieces = [both(x.at[c, f], snaps, i), both(near.at[c, f], HALF, i)]
+            mm[f, l, j + 1] = split_dot(near_w[...], pieces)
+        return carry
+
+    lax.fori_loop(0, cells, near_part, 0, unroll=8)
+    for c in range(2, chunks):
+        compact(c)
+        if c < DEPTH:
+            start_far(c)
+    for c in range(1, DEPTH):
+        pass_on(c)
+
+    for side in range(2):
+
+        @pl.when(receives[side])
+        def _():
+            edge_copy(side).wait_recv()
+
+    edge_mean[...] = dot(own_w, edge[...]) + dot(
+        halo_w, jnp.concatenate([edge_halo[0], edge_halo[1]], axis=0)
+    )
+    for side in range(2):
+
+        @pl.when(z_sends[side])
+        def _():
+            mean_copy(side).start()
+
+    wide = lax.broadcasted_iota(jnp.int32, (snaps, width), 1)
+
+    def spread(r, blocks):
+        l, j = r // rows, lax.rem(r, rows)
+        size = blocks[0].shape[1]
+        split = []
+        for block in blocks:
+            split.extend(halves(block))
+        out = jnp.dot(
+            jnp.concatenate(split, axis=0).astype(jnp.bfloat16), place[r, :size], preferred_element_type=jnp.float32
+        ).astype(jnp.bfloat16)
+        mask = wet[r]
+        for f in range(2):
+            both_halves = jnp.dot(
+                far_w[...], out[2 * f * HALF : 2 * (f + 1) * HALF], preferred_element_type=jnp.float32
+            )
+            mm[f, l, j + 1] = (mm[f, l, j + 1] + both_halves[:snaps] + both_halves[snaps:]) * mask
+
+    def far_part(c):
+        start, _ = tiles(c)
+        if c < per_level:
+
+            def body(m, carry):
+                base = start + 3 * m
+                for k in range(2):
+                    spread(
+                        c * CHUNK + 2 * m + k,
+                        [jnp.concatenate([far[f, base + k], far[f, base + k + 1]], axis=1) for f in range(2)],
+                    )
+                return carry
+
+            lax.fori_loop(0, CHUNK // 2, body, 0, unroll=2)
+        else:
+
+            def body(i, carry):
+                spread(c * CHUNK + i, [far[f, start + i] for f in range(2)])
+                return carry
+
+            lax.fori_loop(0, CHUNK, body, 0, unroll=4)
+
+    def grad_x(f, r, masked, scale):
+        q = (2 + f) * cells + r
+        before = pltpu.roll(edge_in[0], lax.rem(2 * LANES - q, LANES), 1)
+        q = f * cells + r
+        after = pltpu.roll(edge_in[1], lax.rem(2 * LANES - 1 - q, LANES), 1)
+        before = jnp.concatenate([before, before], axis=1)
+        after = jnp.concatenate([after, after], axis=1)
+        behind = jnp.where(wide == 0, before, pltpu.roll(masked, 1, 1))
+        ahead = jnp.where(wide == width - 1, after, pltpu.roll(masked, width - 1, 1))
+        return (ahead - behind) * scale
+
+    def convert(l):
+        def body(j, carry):
+            r = l * rows + j
+            c, i = r // CHUNK, lax.rem(r, CHUNK)
+            mask = wet[r]
+            scale_x = cx[j]
+            scale_y = cy[j]
+            eddy, gx, gy = [], [], []
+            for f in range(2):
+                masked = mm[f, l, j + 1]
+                eddy.append(both(x.at[c, f], snaps, i) - masked)
+                gx.append(grad_x(f, r, masked, scale_x))
+                gy.append((mm[f, l, j + 2] - mm[f, l, j]) * scale_y)
+            eu, ev = eddy
+            total = eu * eu * gx[0] + eu * ev * (gy[0] + gx[1]) + ev * ev * gy[1]
+            conversion = -mask * total
+            for h in range(2):
+                cf.at[c, h].reshape(snaps * CHUNK, LANES)[pl.ds(i, snaps, stride=CHUNK), :] = conversion[
+                    :, h * LANES : (h + 1) * LANES
+                ]
+            part[t, r] = jnp.sum(conversion, axis=0, keepdims=True)
+            return carry
+
+        return body
+
+    def finish(c):
+        for k in range(1, n_tm):
+            part_copy(c, k, lax.rem(t + n_tm - k, n_tm)).wait_recv()
+        l, low, high = converted(c)
+        for j in range(low, high):
+            total = part[0, l * rows + j]
+            for s in range(1, n_tm):
+                total = total + part[s, l * rows + j]
+            mean_ref[l, j : j + 1, :] = total / (snaps * n_tm)
+
+    for c in range(chunks):
+        @pl.when(has_far)
+        def _():
+            for f in range(2):
+                far_copy(c, f).wait_send()
+
+        if c + DEPTH < chunks:
+            start_far(c + DEPTH)
+
+        @pl.when(has_far)
+        def _():
+            for f in range(2):
+                far_copy(c, f).wait_recv()
+
+        far_part(c)
+        if c + DEPTH < chunks:
+            pass_on(c + DEPTH)
+        if c == 0:
+            for side in range(2):
+
+                @pl.when(z_receives[side])
+                def _():
+                    mean_copy(side).wait_recv()
+
+        l, low, high = converted(c)
+        lax.fori_loop(low, high, convert(l), 0, unroll=2)
+        for k in range(1, n_tm):
+            part_copy(c, k, t).start()
+        if c % per_level == per_level - 1:
+
+            def narrow(s, carry):
+                for h in range(2):
+                    block = jnp.concatenate([cf[l * per_level + p, h, s] for p in range(per_level)], axis=0)
+                    conv_ref[s, pl.ds(l * rows, rows), pl.ds(h * LANES, LANES)] = block.astype(jnp.bfloat16)
+                return carry
+
+            lax.fori_loop(0, snaps, narrow, 0, unroll=4)
+
+    for k in range(1, n_tile):
+        flag_copy(k, lax.rem(z + n_tile - k, n_tile)).wait_recv()
+    worst = flags[0]
+    for s in range(1, n_tile):
+        worst = jnp.maximum(worst, flags[s])
+    flag_ref[...] = worst
+    for c in range(chunks):
+        finish(c)
+
+    near_copy().wait_send()
+    for side in range(2):
+
+        @pl.when(sends[side])
+        def _():
+            edge_copy(side).wait_send()
+
+        @pl.when(z_sends[side])
+        def _():
+            mean_copy(side).wait_send()
+
+    @pl.when(at_end)
+    def _():
+        for c in range(chunks):
+            from_relay(c).wait_send()
+
+    for k in range(1, n_tile):
+        flag_copy(k, z).wait_send()
+    for c in range(chunks):
+        for k in range(1, n_tm):
+            part_copy(c, k, t).wait_send()
+
+
+def full(own, halo, velocity_u, velocity_v, land_sea, bottom_level, spacing_x, spacing_y):
+    snaps, cells, width = velocity_u.shape
+    rows = land_sea.shape[0]
+    levels = cells // rows
     n_tm, n_tile = lax.axis_size("tm"), lax.axis_size("tile")
-    assert width == 2 * LANES and 4 * cells == LANES and snaps >= HALF and rows % CHUNK == 0 and n_tm % 4 == 0
-    own, halo = band_parts(snaps)
     chunks = cells // CHUNK
     vmem = pl.BlockSpec(memory_space=pltpu.VMEM)
     hbm = pl.BlockSpec(memory_space=pltpu.HBM)
     f32, bf16 = jnp.float32, jnp.bfloat16
     dma = pltpu.SemaphoreType.DMA
-    conversion, mean_map = pl.pallas_call(
+    return pl.pallas_call(
         functools.partial(kernel, n_tm, n_tile, levels),
         out_shape=(
             jax.ShapeDtypeStruct((snaps, cells, width), bf16),
@@ -515,14 +1024,101 @@
             dma((chunks, n_tm)),
         ],
         compiler_params=pltpu.CompilerParams(
+            collective_id=1, has_side_effects=True, vmem_limit_bytes=60 * 1024 * 1024
+        ),
+        cost_estimate=pl.CostEstimate(flops=10**9, bytes_accessed=4 * 10**6, transcendentals=0),
+    )(
+        velocity_u, velocity_v, land_sea, bottom_level, spacing_x, spacing_y, own, halo,
+    )
+
+
+def quick(own, halo, velocity_u, velocity_v, land_sea, bottom_level, spacing_x, spacing_y):
+    snaps, cells, width = velocity_u.shape
+    rows = land_sea.shape[0]
+    levels = cells // rows
+    n_tm, n_tile = lax.axis_size("tm"), lax.axis_size("tile")
+    chunks = cells // CHUNK
+    packs = rows * 3 // 2 + (levels - 1) * rows
+    vmem = pl.BlockSpec(memory_space=pltpu.VMEM)
+    hbm = pl.BlockSpec(memory_space=pltpu.HBM)
+    f32, bf16 = jnp.float32, jnp.bfloat16
+    dma = pltpu.SemaphoreType.DMA
+    return pl.pallas_call(
+        functools.partial(fast_kernel, n_tm, n_tile, levels),
+        out_shape=(
+            jax.ShapeDtypeStruct((snaps, cells, width), bf16),
+            jax.ShapeDtypeStruct((levels, rows, width), f32),
+            jax.ShapeDtypeStruct((8, LANES), f32),
+        ),
+        in_specs=[hbm] * 8,
+        out_specs=(vmem, vmem, vmem),
+        scratch_shapes=[
+            pltpu.VMEM((rows, width), jnp.int32),
+            pltpu.VMEM((rows, width), jnp.int32),
+            pltpu.VMEM((rows, width), f32),
+            pltpu.VMEM((rows, width), f32),
+            pltpu.VMEM(own.shape, f32),
+            pltpu.VMEM(halo.shape, f32),
+            dma((6,)),
+            pltpu.VMEM((chunks, 2, 2, snaps, CHUNK, LANES), f32),
+            pltpu.VMEM((chunks, 2, 2, HALF, CHUNK, LANES), f32),
+            pltpu.VMEM((2, levels, rows + 2, snaps, width), f32),
+            pltpu.VMEM((chunks, 2, snaps, CHUNK, LANES), f32),
+            pltpu.VMEM((cells, 1, width), f32),
+            pltpu.VMEM((cells, 1, width), f32),
+            pltpu.VMEM((rows, 1, width), f32),
+            pltpu.VMEM((rows, 1, width), f32),
+            pltpu.VMEM((n_tm, cells, 1, width), f32),
+            pltpu.VMEM((snaps, LANES), f32),
+            pltpu.VMEM((2, HALF, LANES), f32),
+            pltpu.VMEM((snaps, LANES), f32),
+            pltpu.VMEM((2, snaps, LANES), f32),
+            pltpu.VMEM((2 * snaps, 2 * (snaps + HALF)), bf16),
+            pltpu.VMEM((2 * snaps, 2 * HALF), bf16),
+            pltpu.VMEM((cells, width, width), bf16),
+            pltpu.VMEM((2, packs, HALF, LANES), f32),
+            pltpu.VMEM((2, packs, HALF, LANES), f32),
+            pltpu.VMEM((packs, HALF, LANES), f32),
+            pltpu.VMEM((n_tile, 8, LANES), f32),
+            dma((chunks,)),
+            dma((chunks,)),
+            dma((chunks, 2, 2)),
+            dma((2,)),
+            dma((chunks, 2)),
+            dma((chunks, 2)),
+            dma((2,)),
+            dma((2,)),
+            dma((2,)),
+            dma((2,)),
+            dma((chunks, n_tm)),
+            dma((chunks, n_tm)),
+            dma((n_tile,)),
+            dma((n_tile,)),
+        ],
+        compiler_params=pltpu.CompilerParams(
             collective_id=0, has_side_effects=True, vmem_limit_bytes=60 * 1024 * 1024
         ),
         cost_estimate=pl.CostEstimate(flops=10**9, bytes_accessed=4 * 10**6, transcendentals=0),
     )(
-        velocity_u.reshape(snaps, cells, width),
-        velocity_v.reshape(snaps, cells, width),
+        velocity_u, velocity_v, land_sea, bottom_level, spacing_x, spacing_y, own, halo,
+    )
+
+
+def shards(velocity_u, velocity_v, land_sea, bottom_level, spacing_x, spacing_y):
+    snaps, levels, rows, width = velocity_u.shape
+    cells = levels * rows
+    n_tm = lax.axis_size("tm")
+    assert width == 2 * LANES and 4 * cells == LANES and snaps == 2 * HALF
+    assert rows % (2 * CHUNK) == 0 and n_tm % 4 == 0 and n_tm >= 8
+    own, halo = band_parts(snaps)
+    args = (
+        jnp.asarray(own), jnp.asarray(halo),
+        velocity_u.reshape(snaps, cells, width), velocity_v.reshape(snaps, cells, width),
         land_sea, bottom_level, spacing_x, spacing_y,
-        jnp.asarray(own), jnp.asarray(halo),
+    )
+    conversion, mean_map, excess = quick(*args)
+    conversion, mean_map = lax.cond(
+        excess[0, LANES - 1] > 0.0, lambda args, done: full(*args), lambda args, done: done, args, (conversion, mean_map)
     )
     return conversion.reshape(velocity_u.shape), mean_map
 

time: 45.6 us -> 38.5 us (0.84)
  Pallas kernels: 42.2 us -> 34.1 us
  between operations: 0.65 us -> 1.43 us
    pallas_call x1, Pallas kernels: 42.2 us -> 34.1 us  [quick(): pl.pallas_call(functools.partial(fast_kernel, n_tm, n_tile, levels), out_...]
    slice x0 -> x1, local copies, waits for them, and re-layouts: none -> 1.25 us  [shards(): excess[0, LANES - 1] > 0.0]
    unnamed x4 -> x18, local copies, waits for them, and re-layouts: 2.69 us -> 1.54 us
where the time goes in v2:
time: 38.5 us; the launch traced here: 38.3 us
  Pallas kernels  34.1 us (89%)
  local copies, waits for them, and re-layouts  2.79 us (7%)
  between operations  1.43 us (4%)
    pallas_call x1, Pallas kernels, quick(): pl.pallas_call(functools.partial(fast_kernel, n_tm, n_tile, levels), out_...  34.1 us
    unnamed x18, local copies, waits for them, and re-layouts  1.54 us
    slice x1, local copies, waits for them, and re-layouts, shards(): excess[0, LANES - 1] > 0.0  1.25 us

profile of v2, /device:TPU:0, one launch (start us, length us, event | category | flops | bytes accessed | tf_op | source)
XLA Modules:
  0.0 38.3 jit_solution(11344435868666048842)
XLA Ops:
  0.6 0.0 copy-start
  0.6 0.0 copy-start.1
  0.7 0.0 copy-start.2
  0.7 0.0 copy-start.3
  0.7 0.0 copy-start.4
  0.7 0.0 copy-start.5
  0.7 0.0 copy-start.6
  0.7 0.0 copy-start.7
  0.7 34.1 %shard_map.95 = (bf16[48,32,256]{2,1,0:T(8,128)(2,1)S(1)}, f32[2,16,256]{2,1,0:T(8,128)S(1)}, f32[8,128]{1,0:T(8,128)}) custom-call(f32[48,32,256]{2,1,0:T(8,128)} %bitcast.5, f32[48,32,256]{2,1,0:T(8,128)} %bitcast.7, s32[16,256]{1,0:T(8,128)} %land_in.1, s32[16,256]{1,0:T(8,128)} %bottom_in.1, f32[16,256]{1,0:T(8,128)} %sx_in.1, f32[16,256]{1,0:T(8,128)} %sy_in.1, ...), custom_call_target="tpu_custom_call" | custom-call | flops 1000000000 | bytes 4000000 | tf_op jit(solution)/shard_map/pallas_call | solution.py:1046
  34.8 1.3 %slice.3 = f32[1,1]{1,0:T(1,128)} slice(f32[8,128]{1,0:T(8,128)} %get-tuple-element.44), slice={[0:1], [127:128]} | slice | bytes 8 | tf_op jit(solution)/shard_map/slice | solution.py:1121
  36.7 0.0 copy-done
  36.7 0.0 copy-done.1
  36.7 0.0 copy-done.2
  36.8 0.0 copy-done.3
  36.8 0.0 copy-done.4
  36.8 0.0 copy-done.5
  36.8 0.0 copy-done.6
  36.8 0.0 copy-done.7
  36.8 0.9 %copy.16 = bf16[48,2,16,256]{3,2,1,0:T(8,128)(2,1)} copy(bf16[48,2,16,256]{3,2,1,0:T(8,128)(2,1)S(1)} %bitcast.4) | data formatting | bytes 1572864
  37.7 0.6 %copy.17 = f32[2,16,256]{2,1,0:T(8,128)} copy(f32[2,16,256]{2,1,0:T(8,128)S(1)} %get-tuple-element.61) | data formatting | bytes 65536
  (1 shorter events, 0.0 us)
Async XLA Ops:
  0.6 36.1 %copy-start = (f32[48,2,16,256]{3,2,1,0:T(8,128)S(1)}, f32[48,2,16,256]{3,2,1,0:T(8,128)}, u32[]{:S(2)}) copy-start(f32[48,2,16,256]{3,2,1,0:T(8,128)} %param.10) | copy-start | bytes 4718596
  0.6 36.1 %copy-start.1 = (f32[48,2,16,256]{3,2,1,0:T(8,128)S(1)}, f32[48,2,16,256]{3,2,1,0:T(8,128)}, u32[]{:S(2)}) copy-start(f32[48,2,16,256]{3,2,1,0:T(8,128)} %param.11) | copy-start | bytes 4718596
  0.7 36.1 %copy-start.2 = (s32[16,256]{1,0:T(8,128)S(1)}, s32[16,256]{1,0:T(8,128)}, u32[]{:S(2)}) copy-start(s32[16,256]{1,0:T(8,128)} %land_in.1) | copy-start | bytes 49156
  0.7 36.1 %copy-start.3 = (s32[16,256]{1,0:T(8,128)S(1)}, s32[16,256]{1,0:T(8,128)}, u32[]{:S(2)}) copy-start(s32[16,256]{1,0:T(8,128)} %bottom_in.1) | copy-start | bytes 49156
  0.7 36.1 %copy-start.4 = (f32[16,256]{1,0:T(8,128)S(1)}, f32[16,256]{1,0:T(8,128)}, u32[]{:S(2)}) copy-start(f32[16,256]{1,0:T(8,128)} %sx_in.1) | copy-start | bytes 49156
  0.7 36.1 %copy-start.5 = (f32[16,256]{1,0:T(8,128)S(1)}, f32[16,256]{1,0:T(8,128)}, u32[]{:S(2)}) copy-start(f32[16,256]{1,0:T(8,128)} %sy_in.1) | copy-start | bytes 49156
  0.7 36.1 %copy-start.6 = (f32[48,48]{1,0:T(8,128)S(1)}, f32[48,48]{1,0:T(8,128)}, u32[]{:S(2)}) copy-start(f32[48,48]{1,0:T(8,128)} %constant.8.clone.halo_in) | copy-start | bytes 27652
  0.7 36.1 %copy-start.7 = (f32[48,48]{1,0:T(8,128)S(1)}, f32[48,48]{1,0:T(8,128)}, u32[]{:S(2)}) copy-start(f32[48,48]{1,0:T(8,128)} %constant.7.clone.own_in) | copy-start | bytes 27652

commit v3 on v2

--- a/solution.py
+++ b/solution.py
@@ -925,7 +925,7 @@
                     mean_copy(side).wait_recv()
 
         l, low, high = converted(c)
-        lax.fori_loop(low, high, convert(l), 0, unroll=2)
+        lax.fori_loop(low, high, convert(l), 0, unroll=4)
         for k in range(1, n_tm):
             part_copy(c, k, t).start()
         if c % per_level == per_level - 1:
@@ -943,7 +943,7 @@
     worst = flags[0]
     for s in range(1, n_tile):
         worst = jnp.maximum(worst, flags[s])
-    flag_ref[...] = worst
+    flag_ref[0] = jnp.max(worst[:, LANES - 1 :])
     for c in range(chunks):
         finish(c)
 
@@ -1048,10 +1048,10 @@
         out_shape=(
             jax.ShapeDtypeStruct((snaps, cells, width), bf16),
             jax.ShapeDtypeStruct((levels, rows, width), f32),
-            jax.ShapeDtypeStruct((8, LANES), f32),
+            jax.ShapeDtypeStruct((1,), f32),
         ),
         in_specs=[hbm] * 8,
-        out_specs=(vmem, vmem, vmem),
+        out_specs=(vmem, vmem, pl.BlockSpec(memory_space=pltpu.SMEM)),
         scratch_shapes=[
             pltpu.VMEM((rows, width), jnp.int32),
             pltpu.VMEM((rows, width), jnp.int32),
@@ -1118,9 +1118,33 @@
     )
     conversion, mean_map, excess = quick(*args)
     conversion, mean_map = lax.cond(
-        excess[0, LANES - 1] > 0.0, lambda args, done: full(*args), lambda args, done: done, args, (conversion, mean_map)
+        excess[0] > 0.0, lambda args, done: full(*args), lambda args, done: done, args, (conversion, mean_map)
     )
+    conversion, mean_map = store(conversion, mean_map)
     return conversion.reshape(velocity_u.shape), mean_map
+
+
+def store_kernel(a_ref, b_ref, a_out, b_out, sem):
+    copies = [
+        pltpu.make_async_copy(a_ref, a_out, sem.at[0]),
+        pltpu.make_async_copy(b_ref, b_out, sem.at[1]),
+    ]
+    for copy in copies:
+        copy.start()
+    for copy in copies:
+        copy.wait()
+
+
+def store(a, b):
+    place = pl.BlockSpec(memory_space=pl.ANY)
+    return pl.pallas_call(
+        store_kernel,
+        out_shape=(jax.ShapeDtypeStruct(a.shape, a.dtype), jax.ShapeDtypeStruct(b.shape, b.dtype)),
+        in_specs=[place, place],
+        out_specs=(pl.BlockSpec(memory_space=pltpu.HBM), pl.BlockSpec(memory_space=pltpu.HBM)),
+        scratch_shapes=[pltpu.SemaphoreType.DMA((2,))],
+        name="store",
+    )(a, b)
 
 
 def solution(mesh):

time: 38.5 us -> 36.3 us (0.943)
  local copies, waits for them, and re-layouts: 2.79 us -> 0.03 us
  Pallas kernels: 34.1 us -> 34.7 us
    unnamed x18 -> x14, local copies, waits for them, and re-layouts: 1.54 us -> 0.03 us
    slice x1 -> x0, local copies, waits for them, and re-layouts: 1.25 us -> none  [shards(): excess[0, LANES - 1] > 0.0]
    pallas_call x0 -> x1, Pallas kernels: none -> 0.9 us  [store(): pl.pallas_call(store_kernel, out_shape=(jax.ShapeDtypeStruct(a.shape, a.d...]
where the time goes in v3:
time: 36.3 us; the launch traced here: 36.2 us
  Pallas kernels  34.7 us (96%)
  between operations  1.38 us (4%)
    pallas_call x1, Pallas kernels, quick(): pl.pallas_call(functools.partial(fast_kernel, n_tm, n_tile, levels), out_...  33.8 us
    pallas_call x1, Pallas kernels, store(): pl.pallas_call(store_kernel, out_shape=(jax.ShapeDtypeStruct(a.shape, a.d...  0.9 us

profile of v3, /device:TPU:0, one launch (start us, length us, event | category | flops | bytes accessed | tf_op | source)
XLA Modules:
  0.0 36.2 jit_solution(16318907836725268208)
XLA Ops:
  0.6 0.0 copy-start
  0.6 0.0 copy-start.1
  0.7 0.0 copy-start.2
  0.7 0.0 copy-start.3
  0.7 0.0 copy-start.4
  0.7 0.0 copy-start.5
  0.7 0.0 copy-start.6
  0.7 33.8 %shard_map.95 = (bf16[48,32,256]{2,1,0:T(8,128)(2,1)S(1)}, f32[2,16,256]{2,1,0:T(8,128)S(1)}, f32[1]{0:T(128)}) custom-call(f32[48,32,256]{2,1,0:T(8,128)} %bitcast.4, f32[48,32,256]{2,1,0:T(8,128)} %bitcast.6, s32[16,256]{1,0:T(8,128)} %land_in.1, s32[16,256]{1,0:T(8,128)} %bottom_in.1, f32[16,256]{1,0:T(8,128)} %sx_in.1, f32[16,256]{1,0:T(8,128)} %sy_in.1, ...), custom_call_target="tpu_custom_call" | custom-call | flops 1000000000 | bytes 4000000 | tf_op jit(solution)/shard_map/pallas_call | solution.py:1046
  35.2 0.0 copy-done
  35.2 0.0 copy-done.1
  35.2 0.0 copy-done.2
  35.2 0.0 copy-done.3
  35.2 0.0 copy-done.4
  35.2 0.0 copy-done.5
  35.2 0.0 copy-done.6
  35.3 0.9 %store.1 = (bf16[48,32,256]{2,1,0:T(8,128)(2,1)}, f32[2,16,256]{2,1,0:T(8,128)}) custom-call(bf16[48,32,256]{2,1,0:T(8,128)(2,1)S(1)} %get-tuple-element.40.a_ref, f32[2,16,256]{2,1,0:T(8,128)S(1)} %get-tuple-element.41.b_ref), custom_call_target="tpu_custom_call" | custom-call | tf_op jit(solution)/shard_map/store/pallas_call | solution.py:1140
  (1 shorter events, 0.0 us)
Async XLA Ops:
  0.6 34.5 %copy-start = (f32[48,2,16,256]{3,2,1,0:T(8,128)S(1)}, f32[48,2,16,256]{3,2,1,0:T(8,128)}, u32[]{:S(2)}) copy-start(f32[48,2,16,256]{3,2,1,0:T(8,128)} %param.10) | copy-start | bytes 4718596
  0.6 34.5 %copy-start.1 = (s32[16,256]{1,0:T(8,128)S(1)}, s32[16,256]{1,0:T(8,128)}, u32[]{:S(2)}) copy-start(s32[16,256]{1,0:T(8,128)} %land_in.1) | copy-start | bytes 49156
  0.7 34.5 %copy-start.2 = (s32[16,256]{1,0:T(8,128)S(1)}, s32[16,256]{1,0:T(8,128)}, u32[]{:S(2)}) copy-start(s32[16,256]{1,0:T(8,128)} %bottom_in.1) | copy-start | bytes 49156
  0.7 34.5 %copy-start.3 = (f32[16,256]{1,0:T(8,128)S(1)}, f32[16,256]{1,0:T(8,128)}, u32[]{:S(2)}) copy-start(f32[16,256]{1,0:T(8,128)} %sx_in.1) | copy-start | bytes 49156
  0.7 34.5 %copy-start.4 = (f32[16,256]{1,0:T(8,128)S(1)}, f32[16,256]{1,0:T(8,128)}, u32[]{:S(2)}) copy-start(f32[16,256]{1,0:T(8,128)} %sy_in.1) | copy-start | bytes 49156
  0.7 34.5 %copy-start.5 = (f32[48,48]{1,0:T(8,128)S(1)}, f32[48,48]{1,0:T(8,128)}, u32[]{:S(2)}) copy-start(f32[48,48]{1,0:T(8,128)} %constant.8.clone.halo_in) | copy-start | bytes 27652
  0.7 34.5 %copy-start.6 = (f32[48,48]{1,0:T(8,128)S(1)}, f32[48,48]{1,0:T(8,128)}, u32[]{:S(2)}) copy-start(f32[48,48]{1,0:T(8,128)} %constant.7.clone.own_in) | copy-start | bytes 27652

commit v4 on v3

--- a/solution.py
+++ b/solution.py
@@ -13,6 +13,9 @@
 LANES = 128
 CHUNK = 8
 DEPTH = 2
+GROUP = 4
+WINDOWS = (((0, 3), (0, 1)), ((1, 5), (1, 3)), ((3, 7), (5, 7)), ((5, 8), (7, 8)))
+SPAN = 2 * GROUP
 MESH = pl.DeviceIdType.MESH
 
 
@@ -474,8 +477,9 @@
     rows = cells // levels
     t = lax.axis_index("tm")
     z = lax.axis_index("tile")
-    chunks = cells // CHUNK
+    blocks = cells // CHUNK
     per_level = rows // CHUNK
+    chunks = rows // GROUP
     fields = (u_ref, v_ref)
     even = lax.rem(t, 2) == 0
     odd = jnp.logical_not(even)
@@ -497,10 +501,11 @@
     )
     for i, (src, dst) in enumerate(small):
         pltpu.make_async_copy(src, dst, small_sem.at[i]).start()
-    for c in range(chunks):
-        for f in range(2):
-            for h in range(2):
-                local(c, f, h).start()
+    for p in range(per_level):
+        for l in range(levels):
+            for f in range(2):
+                for h in range(2):
+                    local(l * per_level + p, f, h).start()
 
     first_far = jnp.where(even, 0, snaps - HALF)
     first_near = jnp.where(even, snaps - HALF, 0)
@@ -512,10 +517,7 @@
     forward_to = jnp.where(t == 0, n_tm // 2 - 1, n_tm // 2)
 
     def tiles(c):
-        wide = CHUNK * 3 // 2
-        l = c // per_level
-        start = c * wide if l == 0 else per_level * wide + (c - per_level) * CHUNK
-        return start, wide if l == 0 else CHUNK
+        return c * SPAN, SPAN
 
     def near_copy():
         return pltpu.make_async_remote_copy(
@@ -613,16 +615,13 @@
         )
 
     def converted(c):
-        piece = c % per_level
-        low = piece * CHUNK - (1 if piece else 0)
-        high = rows if piece == per_level - 1 else (piece + 1) * CHUNK - 1
-        return c // per_level, low, high
+        return c * GROUP - (1 if c else 0), rows if c == chunks - 1 else (c + 1) * GROUP - 1
 
     def part_copy(c, k, slot):
-        l, low, high = converted(c)
-        return pltpu.make_async_remote_copy(
-            src_ref=part.at[slot, pl.ds(l * rows + low, high - low)],
-            dst_ref=part.at[slot, pl.ds(l * rows + low, high - low)],
+        low, high = converted(c)
+        return pltpu.make_async_remote_copy(
+            src_ref=part.at[slot, pl.ds(levels * low, levels * (high - low))],
+            dst_ref=part.at[slot, pl.ds(levels * low, levels * (high - low))],
             send_sem=part_send.at[c, k],
             recv_sem=part_recv.at[c, k],
             device_id={"tm": lax.rem(t + k, n_tm)},
@@ -644,13 +643,43 @@
     all_wet = jnp.concatenate(levels_wet, axis=0)
     lower = lax.broadcasted_iota(jnp.int32, (width, width), 0)
     upper = lax.broadcasted_iota(jnp.int32, (width, width), 1)
-    before = jnp.where(lower < upper, 1.0, 0.0).astype(jnp.bfloat16)
-    order = jnp.dot(all_wet.astype(jnp.bfloat16), before, preferred_element_type=jnp.float32)
+    earlier = jnp.where(lower < upper, 1.0, 0.0).astype(jnp.bfloat16)
+
+    def ranked(index):
+        j = lax.rem(index, rows)
+        side = lax.rem(j, GROUP) // 2
+        inner = jnp.where(side == 0, lax.rem(j, 2), 1 - lax.rem(j, 2))
+        return 2 * (j // GROUP) + side, 2 * inner + (1 - index // rows)
+
+    set_a, rank_a = ranked(lax.broadcasted_iota(jnp.int32, (cells, cells), 0))
+    set_b, rank_b = ranked(lax.broadcasted_iota(jnp.int32, (cells, cells), 1))
+    ahead_rows = jnp.where((set_a == set_b) & (rank_b < rank_a), 1.0, 0.0).astype(jnp.bfloat16)
+    same_rows = jnp.where((set_a // 2 == set_b // 2) & (set_a != set_b), 1.0, 0.0).astype(jnp.bfloat16)
+    wet_bits = all_wet.astype(jnp.bfloat16)
+    filled = jnp.dot(
+        jnp.concatenate([ahead_rows, same_rows], axis=0), wet_bits, preferred_element_type=jnp.float32
+    ).astype(jnp.bfloat16)
+    every = jnp.ones((width, width), jnp.bfloat16)
+    order = jnp.dot(wet_bits, earlier, preferred_element_type=jnp.float32) + jnp.dot(
+        filled[:cells], every, preferred_element_type=jnp.float32
+    )
+    other = jnp.dot(filled[cells:], every, preferred_element_type=jnp.float32)
     row = lax.broadcasted_iota(jnp.int32, (cells, width), 0)
-    room = jnp.where(row < rows, float(width * 3 // 4), float(width // 2))
-    shift = jnp.where((row < rows) & (lax.rem(row, 2) == 1), float(width // 4), 0.0)
-    all_key = jnp.where((all_wet > 0.0) & (order < room), order + shift, -1.0)
-    over = jnp.max(order + all_wet - room, axis=0, keepdims=True)
+    right = lax.rem(lax.rem(row, rows), GROUP) >= 2
+    spot = jnp.where(right, float(SPAN * LANES - 1) - order, order)
+    first_lane = jnp.zeros((cells, width), jnp.float32)
+    lanes_used = jnp.zeros((cells, width), jnp.float32)
+    for q in range(GROUP):
+        for l in range(levels):
+            here = (lax.rem(lax.rem(row, rows), GROUP) == q) & (row // rows == l)
+            low, high = WINDOWS[q][l]
+            first_lane = jnp.where(here, float(low * LANES), first_lane)
+            lanes_used = jnp.where(here, float((high - low) * LANES), lanes_used)
+    spot = spot - first_lane
+    fits = (spot >= 0.0) & (spot < lanes_used) & (order + other < float(SPAN * LANES))
+    is_wet = all_wet > 0.0
+    all_key = jnp.where(is_wet & fits, spot, -1.0)
+    over = jnp.max(jnp.where(is_wet & jnp.logical_not(fits), 1.0, 0.0), axis=0, keepdims=True)
     flags[z] = jnp.broadcast_to(jnp.maximum(over[:, :LANES], over[:, LANES:]), (8, LANES))
     for r in range(cells):
         wet[r] = all_wet[r : r + 1, :]
@@ -662,65 +691,59 @@
     def both(ref, count, j):
         return jnp.concatenate([series(ref.at[h], count, j) for h in range(2)], axis=1)
 
-    def put(size):
+    def members(c):
+        for q in range(GROUP):
+            for l in range(levels):
+                low, high = WINDOWS[q][l]
+                j = c * GROUP + q
+                yield l * rows + j, l * per_level + j // CHUNK, j % CHUNK, low, high
+
+    def put(r, size):
         index = lax.broadcasted_iota(jnp.int32, (size, width), 0).astype(jnp.float32)
-
-        def body(r, carry):
-            place[r, :size] = jnp.where(index == key[r], 1.0, 0.0).astype(jnp.bfloat16)
-            return carry
-
-        return body
-
-    def gather(c, i, size):
+        place[r, :size] = jnp.where(index == key[r], 1.0, 0.0).astype(jnp.bfloat16)
+
+    def gather(r, b, i, size):
         split = []
         for f in range(2):
-            block = [x.at[c, f, h].reshape(snaps * CHUNK, LANES) for h in range(2)]
+            block = [x.at[b, f, h].reshape(snaps * CHUNK, LANES) for h in range(2)]
             at = pl.ds(first_far * CHUNK + i, HALF, stride=CHUNK)
-            split.extend(halves(jnp.concatenate([b[at, :] for b in block], axis=1)))
+            split.extend(halves(jnp.concatenate([p[at, :] for p in block], axis=1)))
         split = jnp.concatenate(split, axis=0).astype(jnp.bfloat16)
         out = lax.dot_general(
-            split, place[c * CHUNK + i, :size], (((1,), (1,)), ((), ())), preferred_element_type=jnp.float32
+            split, place[r, :size], (((1,), (1,)), ((), ())), preferred_element_type=jnp.float32
         )
         return [out[2 * f * HALF : (2 * f + 1) * HALF] + out[(2 * f + 1) * HALF : (2 * f + 2) * HALF] for f in range(2)]
 
     def compact(c):
-        start, _ = tiles(c)
-        if c < per_level:
-            lax.fori_loop(c * CHUNK, (c + 1) * CHUNK, put(width), 0, unroll=2)
-
-            def body(m, carry):
-                one, two = gather(c, 2 * m, width), gather(c, 2 * m + 1, width)
-                for f in range(2):
-                    packed[f, start + 3 * m] = one[f][:, :LANES]
-                    packed[f, start + 3 * m + 1] = one[f][:, LANES:] + two[f][:, :LANES]
-                    packed[f, start + 3 * m + 2] = two[f][:, LANES:]
-                return carry
-
-            lax.fori_loop(0, CHUNK // 2, body, 0, unroll=2)
-        else:
-            lax.fori_loop(c * CHUNK, (c + 1) * CHUNK, put(LANES), 0, unroll=4)
-
-            def body(i, carry):
-                one = gather(c, i, LANES)
-                for f in range(2):
-                    packed[f, start + i] = one[f]
-                return carry
-
-            lax.fori_loop(0, CHUNK, body, 0, unroll=4)
+        start, count = tiles(c)
+        for r, _, _, low, high in members(c):
+            put(r, (high - low) * LANES)
+        sums = [[None] * count for f in range(2)]
+        for r, b, i, low, high in members(c):
+            values = gather(r, b, i, (high - low) * LANES)
+            for f in range(2):
+                for p in range(low, high):
+                    piece = values[f][:, (p - low) * LANES : (p - low + 1) * LANES]
+                    sums[f][p] = piece if sums[f][p] is None else sums[f][p] + piece
+        for f in range(2):
+            for p in range(count):
+                packed[f, start + p] = sums[f][p]
 
     def wait_local(c):
         for f in range(2):
             for h in range(2):
                 local(c, f, h).wait()
 
-    wait_local(0)
+    for l in range(levels):
+        wait_local(l * per_level)
     compact(0)
     pl.semaphore_wait(barrier, n_tm - 1 + n_tile - 1)
     start_far(0)
     for k in range(1, n_tile):
         flag_copy(k, z).start()
-    for c in range(1, chunks):
-        wait_local(c)
+    for l in range(levels):
+        for p in range(1, per_level):
+            wait_local(l * per_level + p)
     near_copy().start()
     compact(1)
     if DEPTH > 1:
@@ -817,7 +840,7 @@
     wide = lax.broadcasted_iota(jnp.int32, (snaps, width), 1)
 
     def spread(r, blocks):
-        l, j = r // rows, lax.rem(r, rows)
+        l, j = r // rows, r % rows
         size = blocks[0].shape[1]
         split = []
         for block in blocks:
@@ -834,25 +857,10 @@
 
     def far_part(c):
         start, _ = tiles(c)
-        if c < per_level:
-
-            def body(m, carry):
-                base = start + 3 * m
-                for k in range(2):
-                    spread(
-                        c * CHUNK + 2 * m + k,
-                        [jnp.concatenate([far[f, base + k], far[f, base + k + 1]], axis=1) for f in range(2)],
-                    )
-                return carry
-
-            lax.fori_loop(0, CHUNK // 2, body, 0, unroll=2)
-        else:
-
-            def body(i, carry):
-                spread(c * CHUNK + i, [far[f, start + i] for f in range(2)])
-                return carry
-
-            lax.fori_loop(0, CHUNK, body, 0, unroll=4)
+        for r, _, _, low, high in members(c):
+            spread(
+                r, [jnp.concatenate([far[f, start + p] for p in range(low, high)], axis=1) for f in range(2)]
+            )
 
     def grad_x(f, r, masked, scale):
         q = (2 + f) * cells + r
@@ -865,8 +873,9 @@
         ahead = jnp.where(wide == width - 1, after, pltpu.roll(masked, width - 1, 1))
         return (ahead - behind) * scale
 
-    def convert(l):
-        def body(j, carry):
+    def convert(low, count):
+        def body(q, carry):
+            l, j = q // count, low + lax.rem(q, count)
             r = l * rows + j
             c, i = r // CHUNK, lax.rem(r, CHUNK)
             mask = wet[r]
@@ -885,7 +894,7 @@
                 cf.at[c, h].reshape(snaps * CHUNK, LANES)[pl.ds(i, snaps, stride=CHUNK), :] = conversion[
                     :, h * LANES : (h + 1) * LANES
                 ]
-            part[t, r] = jnp.sum(conversion, axis=0, keepdims=True)
+            part[t, levels * j + l] = jnp.sum(conversion, axis=0, keepdims=True)
             return carry
 
         return body
@@ -893,12 +902,13 @@
     def finish(c):
         for k in range(1, n_tm):
             part_copy(c, k, lax.rem(t + n_tm - k, n_tm)).wait_recv()
-        l, low, high = converted(c)
+        low, high = converted(c)
         for j in range(low, high):
-            total = part[0, l * rows + j]
-            for s in range(1, n_tm):
-                total = total + part[s, l * rows + j]
-            mean_ref[l, j : j + 1, :] = total / (snaps * n_tm)
+            for l in range(levels):
+                total = part[0, levels * j + l]
+                for s in range(1, n_tm):
+                    total = total + part[s, levels * j + l]
+                mean_ref[l, j : j + 1, :] = total / (snaps * n_tm)
 
     for c in range(chunks):
         @pl.when(has_far)
@@ -924,26 +934,25 @@
                 def _():
                     mean_copy(side).wait_recv()
 
-        l, low, high = converted(c)
-        lax.fori_loop(low, high, convert(l), 0, unroll=4)
+        low, high = converted(c)
+        lax.fori_loop(0, levels * (high - low), convert(low, high - low), 0, unroll=high - low)
         for k in range(1, n_tm):
             part_copy(c, k, t).start()
-        if c % per_level == per_level - 1:
-
-            def narrow(s, carry):
-                for h in range(2):
-                    block = jnp.concatenate([cf[l * per_level + p, h, s] for p in range(per_level)], axis=0)
-                    conv_ref[s, pl.ds(l * rows, rows), pl.ds(h * LANES, LANES)] = block.astype(jnp.bfloat16)
-                return carry
-
-            lax.fori_loop(0, snaps, narrow, 0, unroll=4)
-
+
+    def narrow(s, carry):
+        for l in range(levels):
+            for h in range(2):
+                block = jnp.concatenate([cf[l * per_level + p, h, s] for p in range(per_level)], axis=0)
+                conv_ref[s, pl.ds(l * rows, rows), pl.ds(h * LANES, LANES)] = block.astype(jnp.bfloat16)
+        return carry
+
+    lax.fori_loop(0, snaps, narrow, 0, unroll=4)
     for k in range(1, n_tile):
         flag_copy(k, lax.rem(z + n_tile - k, n_tile)).wait_recv()
     worst = flags[0]
     for s in range(1, n_tile):
         worst = jnp.maximum(worst, flags[s])
-    flag_ref[0] = jnp.max(worst[:, LANES - 1 :])
+    flag_ref[0] = jnp.max(worst)
     for c in range(chunks):
         finish(c)
 
@@ -1037,8 +1046,10 @@
     rows = land_sea.shape[0]
     levels = cells // rows
     n_tm, n_tile = lax.axis_size("tm"), lax.axis_size("tile")
-    chunks = cells // CHUNK
-    packs = rows * 3 // 2 + (levels - 1) * rows
+    blocks = cells // CHUNK
+    chunks = rows // GROUP
+    packs = chunks * SPAN
+    most = max(high - low for pair in WINDOWS for low, high in pair) * LANES
     vmem = pl.BlockSpec(memory_space=pltpu.VMEM)
     hbm = pl.BlockSpec(memory_space=pltpu.HBM)
     f32, bf16 = jnp.float32, jnp.bfloat16
@@ -1060,10 +1071,10 @@
             pltpu.VMEM(own.shape, f32),
             pltpu.VMEM(halo.shape, f32),
             dma((6,)),
-            pltpu.VMEM((chunks, 2, 2, snaps, CHUNK, LANES), f32),
-            pltpu.VMEM((chunks, 2, 2, HALF, CHUNK, LANES), f32),
+            pltpu.VMEM((blocks, 2, 2, snaps, CHUNK, LANES), f32),
+            pltpu.VMEM((blocks, 2, 2, HALF, CHUNK, LANES), f32),
             pltpu.VMEM((2, levels, rows + 2, snaps, width), f32),
-            pltpu.VMEM((chunks, 2, snaps, CHUNK, LANES), f32),
+            pltpu.VMEM((blocks, 2, snaps, CHUNK, LANES), f32),
             pltpu.VMEM((cells, 1, width), f32),
             pltpu.VMEM((cells, 1, width), f32),
             pltpu.VMEM((rows, 1, width), f32),
@@ -1075,14 +1086,14 @@
             pltpu.VMEM((2, snaps, LANES), f32),
             pltpu.VMEM((2 * snaps, 2 * (snaps + HALF)), bf16),
             pltpu.VMEM((2 * snaps, 2 * HALF), bf16),
-            pltpu.VMEM((cells, width, width), bf16),
+            pltpu.VMEM((cells, most, width), bf16),
             pltpu.VMEM((2, packs, HALF, LANES), f32),
             pltpu.VMEM((2, packs, HALF, LANES), f32),
             pltpu.VMEM((packs, HALF, LANES), f32),
             pltpu.VMEM((n_tile, 8, LANES), f32),
             dma((chunks,)),
             dma((chunks,)),
-            dma((chunks, 2, 2)),
+            dma((blocks, 2, 2)),
             dma((2,)),
             dma((chunks, 2)),
             dma((chunks, 2)),
@@ -1109,7 +1120,7 @@
     cells = levels * rows
     n_tm = lax.axis_size("tm")
     assert width == 2 * LANES and 4 * cells == LANES and snaps == 2 * HALF
-    assert rows % (2 * CHUNK) == 0 and n_tm % 4 == 0 and n_tm >= 8
+    assert rows % (2 * CHUNK) == 0 and levels == 2 and n_tm % 4 == 0 and n_tm >= 8
     own, halo = band_parts(snaps)
     args = (
         jnp.asarray(own), jnp.asarray(halo),

time: 36.3 us -> 32.8 us (0.904)
  Pallas kernels: 34.7 us -> 30.8 us
    pallas_call x1, Pallas kernels: 33.8 us -> 29.9 us  [quick(): pl.pallas_call(functools.partial(fast_kernel, n_tm, n_tile, levels), out_...]
where the time goes in v4:
time: 32.8 us; the launch traced here: 32.6 us
  Pallas kernels  30.8 us (94%)
  between operations  1.56 us (5%)
    pallas_call x1, Pallas kernels, quick(): pl.pallas_call(functools.partial(fast_kernel, n_tm, n_tile, levels), out_...  29.9 us
    pallas_call x1, Pallas kernels, store(): pl.pallas_call(store_kernel, out_shape=(jax.ShapeDtypeStruct(a.shape, a.d...  0.9 us

profile of v4, /device:TPU:0, one launch (start us, length us, event | category | flops | bytes accessed | tf_op | source)
XLA Modules:
  0.0 32.6 jit_solution(3545224306233964039)
XLA Ops:
  0.6 0.0 copy-start
  0.6 0.0 copy-start.1
  0.7 0.0 copy-start.2
  0.7 0.0 copy-start.3
  0.7 0.0 copy-start.4
  0.7 0.0 copy-start.5
  0.7 0.0 copy-start.6
  0.7 29.9 %shard_map.95 = (bf16[48,32,256]{2,1,0:T(8,128)(2,1)S(1)}, f32[2,16,256]{2,1,0:T(8,128)S(1)}, f32[1]{0:T(128)}) custom-call(f32[48,32,256]{2,1,0:T(8,128)} %bitcast.4, f32[48,32,256]{2,1,0:T(8,128)} %bitcast.6, s32[16,256]{1,0:T(8,128)} %land_in.1, s32[16,256]{1,0:T(8,128)} %bottom_in.1, f32[16,256]{1,0:T(8,128)} %sx_in.1, f32[16,256]{1,0:T(8,128)} %sy_in.1, ...), custom_call_target="tpu_custom_call" | custom-call | flops 1000000000 | bytes 4000000 | tf_op jit(solution)/shard_map/pallas_call | solution.py:1057
  31.2 0.0 copy-done
  31.2 0.0 copy-done.1
  31.3 0.0 copy-done.2
  31.3 0.0 copy-done.3
  31.3 0.0 copy-done.4
  31.3 0.0 copy-done.5
  31.3 0.0 copy-done.6
  31.3 0.2 conditional.1
  31.5 0.9 %store.1 = (bf16[48,32,256]{2,1,0:T(8,128)(2,1)}, f32[2,16,256]{2,1,0:T(8,128)}) custom-call(bf16[48,32,256]{2,1,0:T(8,128)(2,1)S(1)} %get-tuple-element.40.a_ref, f32[2,16,256]{2,1,0:T(8,128)S(1)} %get-tuple-element.41.b_ref), custom_call_target="tpu_custom_call" | custom-call | tf_op jit(solution)/shard_map/store/pallas_call | solution.py:1151
Async XLA Ops:
  0.6 30.6 %copy-start = (f32[48,2,16,256]{3,2,1,0:T(8,128)S(1)}, f32[48,2,16,256]{3,2,1,0:T(8,128)}, u32[]{:S(2)}) copy-start(f32[48,2,16,256]{3,2,1,0:T(8,128)} %param.10) | copy-start | bytes 4718596
  0.6 30.6 %copy-start.1 = (s32[16,256]{1,0:T(8,128)S(1)}, s32[16,256]{1,0:T(8,128)}, u32[]{:S(2)}) copy-start(s32[16,256]{1,0:T(8,128)} %land_in.1) | copy-start | bytes 49156
  0.7 30.6 %copy-start.2 = (s32[16,256]{1,0:T(8,128)S(1)}, s32[16,256]{1,0:T(8,128)}, u32[]{:S(2)}) copy-start(s32[16,256]{1,0:T(8,128)} %bottom_in.1) | copy-start | bytes 49156
  0.7 30.6 %copy-start.3 = (f32[16,256]{1,0:T(8,128)S(1)}, f32[16,256]{1,0:T(8,128)}, u32[]{:S(2)}) copy-start(f32[16,256]{1,0:T(8,128)} %sx_in.1) | copy-start | bytes 49156
  0.7 30.6 %copy-start.4 = (f32[16,256]{1,0:T(8,128)S(1)}, f32[16,256]{1,0:T(8,128)}, u32[]{:S(2)}) copy-start(f32[16,256]{1,0:T(8,128)} %sy_in.1) | copy-start | bytes 49156
  0.7 30.6 %copy-start.5 = (f32[48,48]{1,0:T(8,128)S(1)}, f32[48,48]{1,0:T(8,128)}, u32[]{:S(2)}) copy-start(f32[48,48]{1,0:T(8,128)} %constant.8.clone.halo_in) | copy-start | bytes 27652
  0.7 30.6 %copy-start.6 = (f32[48,48]{1,0:T(8,128)S(1)}, f32[48,48]{1,0:T(8,128)}, u32[]{:S(2)}) copy-start(f32[48,48]{1,0:T(8,128)} %constant.7.clone.own_in) | copy-start | bytes 27652

commit v5 on v4

--- a/solution.py
+++ b/solution.py
@@ -13,6 +13,7 @@
 LANES = 128
 CHUNK = 8
 DEPTH = 2
+AHEAD = 3
 GROUP = 4
 WINDOWS = (((0, 3), (0, 1)), ((1, 5), (1, 3)), ((3, 7), (5, 7)), ((5, 8), (7, 8)))
 SPAN = 2 * GROUP
@@ -715,6 +716,11 @@
         return [out[2 * f * HALF : (2 * f + 1) * HALF] + out[(2 * f + 1) * HALF : (2 * f + 2) * HALF] for f in range(2)]
 
     def compact(c):
+        @pl.when(has_far)
+        def _():
+            compact_far(c)
+
+    def compact_far(c):
         start, count = tiles(c)
         for r, _, _, low, high in members(c):
             put(r, (high - low) * LANES)
@@ -734,25 +740,36 @@
             for h in range(2):
                 local(c, f, h).wait()
 
-    for l in range(levels):
-        wait_local(l * per_level)
+    for c in range(blocks):
+        wait_local(c)
+    lane = lax.broadcasted_iota(jnp.int32, (snaps, LANES), 1)
+
+    def pack(r, acc):
+        c, j = r // CHUNK, lax.rem(r, CHUNK)
+        for f in range(2):
+            q = f * cells + r
+            first = series(x.at[c, f, 0], snaps, j) * wet[r][:, :LANES]
+            acc = jnp.where(lane == q, pltpu.roll(first, q, 1), acc)
+            q = (2 + f) * cells + r
+            last = series(x.at[c, f, 1], snaps, j) * wet[r][:, width - LANES :]
+            acc = jnp.where(lane == q, pltpu.roll(last, lax.rem(q + 1, LANES), 1), acc)
+        return acc
+
     compact(0)
     pl.semaphore_wait(barrier, n_tm - 1 + n_tile - 1)
     start_far(0)
+    edge[...] = lax.fori_loop(0, cells, pack, jnp.zeros((snaps, LANES), jnp.float32), unroll=4)
+    for side in range(2):
+
+        @pl.when(sends[side])
+        def _():
+            edge_copy(side).start()
+
     for k in range(1, n_tile):
         flag_copy(k, z).start()
-    for l in range(levels):
-        for p in range(1, per_level):
-            wait_local(l * per_level + p)
     near_copy().start()
     compact(1)
-    if DEPTH > 1:
-        start_far(1)
-
-    @pl.when(at_end)
-    def _():
-        far[...] = jnp.zeros(far.shape, jnp.float32)
-
+    start_far(1)
     for side in range(2):
 
         @pl.when(jnp.logical_not(receives[side]))
@@ -783,29 +800,24 @@
     near_w[...] = stacked_weights(jnp.concatenate([own_w, near_half], axis=1))
     far_w[...] = stacked_weights(far_half)
 
-    lane = lax.broadcasted_iota(jnp.int32, (snaps, LANES), 1)
-
-    def pack(r, acc):
-        c, j = r // CHUNK, lax.rem(r, CHUNK)
-        for f in range(2):
-            q = f * cells + r
-            first = series(x.at[c, f, 0], snaps, j) * wet[r][:, :LANES]
-            acc = jnp.where(lane == q, pltpu.roll(first, q, 1), acc)
-            q = (2 + f) * cells + r
-            last = series(x.at[c, f, 1], snaps, j) * wet[r][:, width - LANES :]
-            acc = jnp.where(lane == q, pltpu.roll(last, lax.rem(q + 1, LANES), 1), acc)
-        return acc
-
-    edge[...] = lax.fori_loop(0, cells, pack, jnp.zeros((snaps, LANES), jnp.float32), unroll=4)
+    pass_on(0)
     for side in range(2):
 
-        @pl.when(sends[side])
-        def _():
-            edge_copy(side).start()
-
-    pass_on(0)
-    near_copy().wait_recv()
-
+        @pl.when(receives[side])
+        def _():
+            edge_copy(side).wait_recv()
+
+    edge_mean[...] = dot(own_w, edge[...]) + dot(
+        halo_w, jnp.concatenate([edge_halo[0], edge_halo[1]], axis=0)
+    )
+    for side in range(2):
+
+        @pl.when(z_sends[side])
+        def _():
+            mean_copy(side).start()
+
+    compact(2)
+    start_far(2)
     def near_part(r, carry):
         l, j = r // rows, lax.rem(r, rows)
         c, i = r // CHUNK, lax.rem(r, CHUNK)
@@ -814,29 +826,11 @@
             mm[f, l, j + 1] = split_dot(near_w[...], pieces)
         return carry
 
+    near_copy().wait_recv()
     lax.fori_loop(0, cells, near_part, 0, unroll=8)
-    for c in range(2, chunks):
-        compact(c)
-        if c < DEPTH:
-            start_far(c)
-    for c in range(1, DEPTH):
-        pass_on(c)
-
-    for side in range(2):
-
-        @pl.when(receives[side])
-        def _():
-            edge_copy(side).wait_recv()
-
-    edge_mean[...] = dot(own_w, edge[...]) + dot(
-        halo_w, jnp.concatenate([edge_halo[0], edge_halo[1]], axis=0)
-    )
-    for side in range(2):
-
-        @pl.when(z_sends[side])
-        def _():
-            mean_copy(side).start()
-
+    compact(3)
+    pass_on(1)
+    pass_on(2)
     wide = lax.broadcasted_iota(jnp.int32, (snaps, width), 1)
 
     def spread(r, blocks):
@@ -857,10 +851,21 @@
 
     def far_part(c):
         start, _ = tiles(c)
-        for r, _, _, low, high in members(c):
-            spread(
-                r, [jnp.concatenate([far[f, start + p] for p in range(low, high)], axis=1) for f in range(2)]
-            )
+
+        @pl.when(has_far)
+        def _():
+            for f in range(2):
+                far_copy(c, f).wait_recv()
+            for r, _, _, low, high in members(c):
+                spread(
+                    r, [jnp.concatenate([far[f, start + p] for p in range(low, high)], axis=1) for f in range(2)]
+                )
+
+        @pl.when(at_end)
+        def _():
+            for r, _, _, _, _ in members(c):
+                for f in range(2):
+                    mm[f, r // rows, r % rows + 1] = mm[f, r // rows, r % rows + 1] * wet[r]
 
     def grad_x(f, r, masked, scale):
         q = (2 + f) * cells + r
@@ -916,17 +921,12 @@
             for f in range(2):
                 far_copy(c, f).wait_send()
 
-        if c + DEPTH < chunks:
-            start_far(c + DEPTH)
-
-        @pl.when(has_far)
-        def _():
-            for f in range(2):
-                far_copy(c, f).wait_recv()
+        if c + AHEAD < chunks:
+            start_far(c + AHEAD)
 
         far_part(c)
-        if c + DEPTH < chunks:
-            pass_on(c + DEPTH)
+        if c + AHEAD < chunks:
+            pass_on(c + AHEAD)
         if c == 0:
             for side in range(2):
 

time: 32.8 us -> 31.7 us (0.966)
  Pallas kernels: 30.8 us -> 29.7 us
    pallas_call x1, Pallas kernels: 29.9 us -> 28.8 us  [quick(): pl.pallas_call(functools.partial(fast_kernel, n_tm, n_tile, levels), out_...]
where the time goes in v5:
time: 31.7 us; the launch traced here: 31.5 us
  Pallas kernels  29.7 us (94%)
  between operations  1.56 us (5%)
    pallas_call x1, Pallas kernels, quick(): pl.pallas_call(functools.partial(fast_kernel, n_tm, n_tile, levels), out_...  28.8 us
    pallas_call x1, Pallas kernels, store(): pl.pallas_call(store_kernel, out_shape=(jax.ShapeDtypeStruct(a.shape, a.d...  0.9 us

profile of v5, /device:TPU:0, one launch (start us, length us, event | category | flops | bytes accessed | tf_op | source)
XLA Modules:
  0.0 31.5 jit_solution(14371590360218767699)
XLA Ops:
  0.6 0.0 copy-start
  0.6 0.0 copy-start.1
  0.7 0.0 copy-start.2
  0.7 0.0 copy-start.3
  0.7 0.0 copy-start.4
  0.7 0.0 copy-start.5
  0.7 0.0 copy-start.6
  0.7 28.8 %shard_map.95 = (bf16[48,32,256]{2,1,0:T(8,128)(2,1)S(1)}, f32[2,16,256]{2,1,0:T(8,128)S(1)}, f32[1]{0:T(128)}) custom-call(f32[48,32,256]{2,1,0:T(8,128)} %bitcast.4, f32[48,32,256]{2,1,0:T(8,128)} %bitcast.6, s32[16,256]{1,0:T(8,128)} %land_in.1, s32[16,256]{1,0:T(8,128)} %bottom_in.1, f32[16,256]{1,0:T(8,128)} %sx_in.1, f32[16,256]{1,0:T(8,128)} %sy_in.1, ...), custom_call_target="tpu_custom_call" | custom-call | flops 1000000000 | bytes 4000000 | tf_op jit(solution)/shard_map/pallas_call | solution.py:1057
  30.1 0.0 copy-done
  30.1 0.0 copy-done.1
  30.2 0.0 copy-done.2
  30.2 0.0 copy-done.3
  30.2 0.0 copy-done.4
  30.2 0.0 copy-done.5
  30.2 0.0 copy-done.6
  30.2 0.2 conditional.1
  30.4 0.9 %store.1 = (bf16[48,32,256]{2,1,0:T(8,128)(2,1)}, f32[2,16,256]{2,1,0:T(8,128)}) custom-call(bf16[48,32,256]{2,1,0:T(8,128)(2,1)S(1)} %get-tuple-element.40.a_ref, f32[2,16,256]{2,1,0:T(8,128)S(1)} %get-tuple-element.41.b_ref), custom_call_target="tpu_custom_call" | custom-call | tf_op jit(solution)/shard_map/store/pallas_call | solution.py:1151
Async XLA Ops:
  0.6 29.5 %copy-start = (f32[48,2,16,256]{3,2,1,0:T(8,128)S(1)}, f32[48,2,16,256]{3,2,1,0:T(8,128)}, u32[]{:S(2)}) copy-start(f32[48,2,16,256]{3,2,1,0:T(8,128)} %param.10) | copy-start | bytes 4718596
  0.6 29.5 %copy-start.1 = (s32[16,256]{1,0:T(8,128)S(1)}, s32[16,256]{1,0:T(8,128)}, u32[]{:S(2)}) copy-start(s32[16,256]{1,0:T(8,128)} %land_in.1) | copy-start | bytes 49156
  0.7 29.5 %copy-start.2 = (s32[16,256]{1,0:T(8,128)S(1)}, s32[16,256]{1,0:T(8,128)}, u32[]{:S(2)}) copy-start(s32[16,256]{1,0:T(8,128)} %bottom_in.1) | copy-start | bytes 49156
  0.7 29.5 %copy-start.3 = (f32[16,256]{1,0:T(8,128)S(1)}, f32[16,256]{1,0:T(8,128)}, u32[]{:S(2)}) copy-start(f32[16,256]{1,0:T(8,128)} %sx_in.1) | copy-start | bytes 49156
  0.7 29.5 %copy-start.4 = (f32[16,256]{1,0:T(8,128)S(1)}, f32[16,256]{1,0:T(8,128)}, u32[]{:S(2)}) copy-start(f32[16,256]{1,0:T(8,128)} %sy_in.1) | copy-start | bytes 49156
  0.7 29.5 %copy-start.5 = (f32[48,48]{1,0:T(8,128)S(1)}, f32[48,48]{1,0:T(8,128)}, u32[]{:S(2)}) copy-start(f32[48,48]{1,0:T(8,128)} %constant.8.clone.halo_in) | copy-start | bytes 27652
  0.7 29.5 %copy-start.6 = (f32[48,48]{1,0:T(8,128)S(1)}, f32[48,48]{1,0:T(8,128)}, u32[]{:S(2)}) copy-start(f32[48,48]{1,0:T(8,128)} %constant.7.clone.own_in) | copy-start | bytes 27652

commit v6 on v5

--- a/solution.py
+++ b/solution.py
@@ -470,7 +470,7 @@
     conv_ref, mean_ref, flag_ref,
     land_ref, bottom_ref, sx_ref, sy_ref, own_ref, halo_w_ref, small_sem,
     x, near, mm, cf, wet, key, cx, cy, part, edge, edge_halo, edge_mean, edge_in,
-    near_w, far_w, place, packed, far, relayed, flags,
+    near_w, far_w, place, packed, far, relayed, flags, flags_in,
     relay_send, relay_recv, x_sem, near_sem, far_send, far_recv, edge_send, edge_recv, em_send, em_recv,
     part_send, part_recv, flag_send, flag_recv,
 ):
@@ -488,8 +488,14 @@
     barrier = pltpu.get_barrier_semaphore()
     for k in range(1, n_tm):
         pl.semaphore_signal(barrier, inc=1, device_id={"tm": lax.rem(t + k, n_tm)}, device_id_type=MESH)
-    for k in range(1, n_tile):
-        pl.semaphore_signal(barrier, inc=1, device_id={"tile": lax.rem(z + k, n_tile)}, device_id_type=MESH)
+    @pl.when(z > 0)
+    def _():
+        pl.semaphore_signal(barrier, inc=1, device_id={"tile": z - 1}, device_id_type=MESH)
+
+    @pl.when(z < n_tile - 1)
+    def _():
+        pl.semaphore_signal(barrier, inc=1, device_id={"tile": z + 1}, device_id_type=MESH)
+
 
     def local(c, f, h):
         return pltpu.make_async_copy(
@@ -605,15 +611,32 @@
             device_id_type=MESH,
         )
 
-    def flag_copy(k, slot):
-        return pltpu.make_async_remote_copy(
-            src_ref=flags.at[slot],
-            dst_ref=flags.at[slot],
-            send_sem=flag_send.at[k],
-            recv_sem=flag_recv.at[k],
-            device_id={"tile": lax.rem(z + k, n_tile)},
-            device_id_type=MESH,
-        )
+    def flag_copy(s, side):
+        to = z + 1 if side == 0 else z - 1
+        return pltpu.make_async_remote_copy(
+            src_ref=flags.at[s],
+            dst_ref=flags_in.at[side, s],
+            send_sem=flag_send.at[s, side],
+            recv_sem=flag_recv.at[s, side],
+            device_id={"tile": to},
+            device_id_type=MESH,
+        )
+
+    def start_flag(s):
+        for side in range(2):
+
+            @pl.when(z_sends[side])
+            def _():
+                flag_copy(s, side).start()
+
+    def finish_flag(s):
+        for side in range(2):
+
+            @pl.when(z_receives[side])
+            def _():
+                flag_copy(s, side).wait_recv()
+
+        flags[s + 1] = jnp.maximum(flags[s], jnp.maximum(flags_in[0, s], flags_in[1, s]))
 
     def converted(c):
         return c * GROUP - (1 if c else 0), rows if c == chunks - 1 else (c + 1) * GROUP - 1
@@ -681,7 +704,7 @@
     is_wet = all_wet > 0.0
     all_key = jnp.where(is_wet & fits, spot, -1.0)
     over = jnp.max(jnp.where(is_wet & jnp.logical_not(fits), 1.0, 0.0), axis=0, keepdims=True)
-    flags[z] = jnp.broadcast_to(jnp.maximum(over[:, :LANES], over[:, LANES:]), (8, LANES))
+    flags[0] = jnp.broadcast_to(jnp.maximum(over[:, :LANES], over[:, LANES:]), (8, LANES))
     for r in range(cells):
         wet[r] = all_wet[r : r + 1, :]
         key[r] = all_key[r : r + 1, :]
@@ -756,7 +779,7 @@
         return acc
 
     compact(0)
-    pl.semaphore_wait(barrier, n_tm - 1 + n_tile - 1)
+    pl.semaphore_wait(barrier, n_tm - 1 + jnp.where(z > 0, 1, 0) + jnp.where(z < n_tile - 1, 1, 0))
     start_far(0)
     edge[...] = lax.fori_loop(0, cells, pack, jnp.zeros((snaps, LANES), jnp.float32), unroll=4)
     for side in range(2):
@@ -765,8 +788,7 @@
         def _():
             edge_copy(side).start()
 
-    for k in range(1, n_tile):
-        flag_copy(k, z).start()
+    start_flag(0)
     near_copy().start()
     compact(1)
     start_far(1)
@@ -779,6 +801,7 @@
         @pl.when(jnp.logical_not(z_receives[side]))
         def _():
             edge_in[side] = jnp.zeros(edge_in.shape[1:], jnp.float32)
+            flags_in[side] = jnp.zeros(flags_in.shape[1:], jnp.float32)
 
     all_x, all_y = 0.5 / sx_ref[...], 0.5 / sy_ref[...]
     for j in range(rows):
@@ -826,6 +849,10 @@
             mm[f, l, j + 1] = split_dot(near_w[...], pieces)
         return carry
 
+    if 0 < n_tile - 1:
+        finish_flag(0)
+    if 0 + 1 < n_tile - 1:
+        start_flag(0 + 1)
     near_copy().wait_recv()
     lax.fori_loop(0, cells, near_part, 0, unroll=8)
     compact(3)
@@ -867,15 +894,15 @@
                 for f in range(2):
                     mm[f, r // rows, r % rows + 1] = mm[f, r // rows, r % rows + 1] * wet[r]
 
-    def grad_x(f, r, masked, scale):
+    wide = lax.broadcasted_iota(jnp.int32, (8, width), 1)
+
+    def grad_x(f, r, now, masked, scale):
         q = (2 + f) * cells + r
-        before = pltpu.roll(edge_in[0], lax.rem(2 * LANES - q, LANES), 1)
+        behind = pltpu.roll(edge_in[0, now, :], lax.rem(2 * LANES - q, LANES), 1)
         q = f * cells + r
-        after = pltpu.roll(edge_in[1], lax.rem(2 * LANES - 1 - q, LANES), 1)
-        before = jnp.concatenate([before, before], axis=1)
-        after = jnp.concatenate([after, after], axis=1)
-        behind = jnp.where(wide == 0, before, pltpu.roll(masked, 1, 1))
-        ahead = jnp.where(wide == width - 1, after, pltpu.roll(masked, width - 1, 1))
+        ahead = pltpu.roll(edge_in[1, now, :], lax.rem(2 * LANES - 1 - q, LANES), 1)
+        behind = jnp.where(wide == 0, jnp.concatenate([behind, behind], axis=1), pltpu.roll(masked, 1, 1))
+        ahead = jnp.where(wide == width - 1, jnp.concatenate([ahead, ahead], axis=1), pltpu.roll(masked, width - 1, 1))
         return (ahead - behind) * scale
 
     def convert(low, count):
@@ -883,23 +910,28 @@
             l, j = q // count, low + lax.rem(q, count)
             r = l * rows + j
             c, i = r // CHUNK, lax.rem(r, CHUNK)
-            mask = wet[r]
+            mask = -wet[r]
             scale_x = cx[j]
             scale_y = cy[j]
-            eddy, gx, gy = [], [], []
-            for f in range(2):
-                masked = mm[f, l, j + 1]
-                eddy.append(both(x.at[c, f], snaps, i) - masked)
-                gx.append(grad_x(f, r, masked, scale_x))
-                gy.append((mm[f, l, j + 2] - mm[f, l, j]) * scale_y)
-            eu, ev = eddy
-            total = eu * eu * gx[0] + eu * ev * (gy[0] + gx[1]) + ev * ev * gy[1]
-            conversion = -mask * total
-            for h in range(2):
-                cf.at[c, h].reshape(snaps * CHUNK, LANES)[pl.ds(i, snaps, stride=CHUNK), :] = conversion[
-                    :, h * LANES : (h + 1) * LANES
-                ]
-            part[t, levels * j + l] = jnp.sum(conversion, axis=0, keepdims=True)
+            kept = jnp.zeros((CHUNK, width), jnp.float32)
+            for first in range(0, snaps, 8):
+                now = pl.ds(first, 8)
+                at = pl.ds(first * CHUNK + i, 8, stride=CHUNK)
+                eddy, gx, gy = [], [], []
+                for f in range(2):
+                    masked = mm[f, l, j + 1, now, :]
+                    raw = [x.at[c, f, h].reshape(snaps * CHUNK, LANES)[at, :] for h in range(2)]
+                    eddy.append(jnp.concatenate(raw, axis=1) - masked)
+                    gx.append(grad_x(f, r, now, masked, scale_x))
+                    gy.append((mm[f, l, j + 2, now, :] - mm[f, l, j, now, :]) * scale_y)
+                eu, ev = eddy
+                total = eu * eu * gx[0] + eu * ev * (gy[0] + gx[1]) + ev * ev * gy[1]
+                conversion = mask * total
+                for h in range(2):
+                    cf.at[c, h].reshape(snaps * CHUNK, LANES)[at, :] = conversion[:, h * LANES : (h + 1) * LANES]
+                for k in range(0, 8, CHUNK):
+                    kept = kept + conversion[k : k + CHUNK]
+            part[t, levels * j + l] = jnp.sum(kept, axis=0, keepdims=True)
             return carry
 
         return body
@@ -915,6 +947,10 @@
                     total = total + part[s, levels * j + l]
                 mean_ref[l, j : j + 1, :] = total / (snaps * n_tm)
 
+    if 1 < n_tile - 1:
+        finish_flag(1)
+    if 1 + 1 < n_tile - 1:
+        start_flag(1 + 1)
     for c in range(chunks):
         @pl.when(has_far)
         def _():
@@ -935,7 +971,7 @@
                     mean_copy(side).wait_recv()
 
         low, high = converted(c)
-        lax.fori_loop(0, levels * (high - low), convert(low, high - low), 0, unroll=high - low)
+        lax.fori_loop(0, levels * (high - low), convert(low, high - low), 0, unroll=2 * (high - low))
         for k in range(1, n_tm):
             part_copy(c, k, t).start()
 
@@ -947,12 +983,11 @@
         return carry
 
     lax.fori_loop(0, snaps, narrow, 0, unroll=4)
-    for k in range(1, n_tile):
-        flag_copy(k, lax.rem(z + n_tile - k, n_tile)).wait_recv()
-    worst = flags[0]
-    for s in range(1, n_tile):
-        worst = jnp.maximum(worst, flags[s])
-    flag_ref[0] = jnp.max(worst)
+    for s in range(2, n_tile - 1):
+        finish_flag(s)
+        if s + 1 < n_tile - 1:
+            start_flag(s + 1)
+    flag_ref[0] = jnp.max(flags[n_tile - 1])
     for c in range(chunks):
         finish(c)
 
@@ -972,8 +1007,13 @@
         for c in range(chunks):
             from_relay(c).wait_send()
 
-    for k in range(1, n_tile):
-        flag_copy(k, z).wait_send()
+    for s in range(n_tile - 1):
+        for side in range(2):
+
+            @pl.when(z_sends[side])
+            def _():
+                flag_copy(s, side).wait_send()
+
     for c in range(chunks):
         for k in range(1, n_tm):
             part_copy(c, k, t).wait_send()
@@ -1091,6 +1131,7 @@
             pltpu.VMEM((2, packs, HALF, LANES), f32),
             pltpu.VMEM((packs, HALF, LANES), f32),
             pltpu.VMEM((n_tile, 8, LANES), f32),
+            pltpu.VMEM((2, n_tile - 1, 8, LANES), f32),
             dma((chunks,)),
             dma((chunks,)),
             dma((blocks, 2, 2)),
@@ -1103,8 +1144,8 @@
             dma((2,)),
             dma((chunks, n_tm)),
             dma((chunks, n_tm)),
-            dma((n_tile,)),
-            dma((n_tile,)),
+            dma((n_tile - 1, 2)),
+            dma((n_tile - 1, 2)),
         ],
         compiler_params=pltpu.CompilerParams(
             collective_id=0, has_side_effects=True, vmem_limit_bytes=60 * 1024 * 1024

time: 31.7 us -> 30.6 us (0.965)
  Pallas kernels: 29.7 us -> 28.6 us
    pallas_call x1, Pallas kernels: 28.8 us -> 27.7 us  [quick(): pl.pallas_call(functools.partial(fast_kernel, n_tm, n_tile, levels), out_...]
where the time goes in v6:
time: 30.6 us; the launch traced here: 30.4 us
  Pallas kernels  28.6 us (93%)
  between operations  1.56 us (5%)
    pallas_call x1, Pallas kernels, quick(): pl.pallas_call(functools.partial(fast_kernel, n_tm, n_tile, levels), out_...  27.7 us
    pallas_call x1, Pallas kernels, store(): pl.pallas_call(store_kernel, out_shape=(jax.ShapeDtypeStruct(a.shape, a.d...  0.9 us

profile of v6, /device:TPU:0, one launch (start us, length us, event | category | flops | bytes accessed | tf_op | source)
XLA Modules:
  0.0 30.4 jit_solution(11140609342467102351)
XLA Ops:
  0.6 0.0 copy-start
  0.6 0.0 copy-start.1
  0.7 0.0 copy-start.2
  0.7 0.0 copy-start.3
  0.7 0.0 copy-start.4
  0.7 0.0 copy-start.5
  0.7 0.0 copy-start.6
  0.7 27.7 %shard_map.95 = (bf16[48,32,256]{2,1,0:T(8,128)(2,1)S(1)}, f32[2,16,256]{2,1,0:T(8,128)S(1)}, f32[1]{0:T(128)}) custom-call(f32[48,32,256]{2,1,0:T(8,128)} %bitcast.4, f32[48,32,256]{2,1,0:T(8,128)} %bitcast.6, s32[16,256]{1,0:T(8,128)} %land_in.1, s32[16,256]{1,0:T(8,128)} %bottom_in.1, f32[16,256]{1,0:T(8,128)} %sx_in.1, f32[16,256]{1,0:T(8,128)} %sy_in.1, ...), custom_call_target="tpu_custom_call" | custom-call | flops 1000000000 | bytes 4000000 | tf_op jit(solution)/shard_map/pallas_call | solution.py:1097
  29.1 0.0 copy-done
  29.1 0.0 copy-done.1
  29.1 0.0 copy-done.2
  29.1 0.0 copy-done.3
  29.1 0.0 copy-done.4
  29.1 0.0 copy-done.5
  29.1 0.0 copy-done.6
  29.1 0.2 conditional.1
  29.4 0.9 %store.1 = (bf16[48,32,256]{2,1,0:T(8,128)(2,1)}, f32[2,16,256]{2,1,0:T(8,128)}) custom-call(bf16[48,32,256]{2,1,0:T(8,128)(2,1)S(1)} %get-tuple-element.40.a_ref, f32[2,16,256]{2,1,0:T(8,128)S(1)} %get-tuple-element.41.b_ref), custom_call_target="tpu_custom_call" | custom-call | tf_op jit(solution)/shard_map/store/pallas_call | solution.py:1192
Async XLA Ops:
  0.6 28.4 %copy-start = (f32[48,2,16,256]{3,2,1,0:T(8,128)S(1)}, f32[48,2,16,256]{3,2,1,0:T(8,128)}, u32[]{:S(2)}) copy-start(f32[48,2,16,256]{3,2,1,0:T(8,128)} %param.10) | copy-start | bytes 4718596
  0.6 28.4 %copy-start.1 = (s32[16,256]{1,0:T(8,128)S(1)}, s32[16,256]{1,0:T(8,128)}, u32[]{:S(2)}) copy-start(s32[16,256]{1,0:T(8,128)} %land_in.1) | copy-start | bytes 49156
  0.7 28.4 %copy-start.2 = (s32[16,256]{1,0:T(8,128)S(1)}, s32[16,256]{1,0:T(8,128)}, u32[]{:S(2)}) copy-start(s32[16,256]{1,0:T(8,128)} %bottom_in.1) | copy-start | bytes 49156
  0.7 28.4 %copy-start.3 = (f32[16,256]{1,0:T(8,128)S(1)}, f32[16,256]{1,0:T(8,128)}, u32[]{:S(2)}) copy-start(f32[16,256]{1,0:T(8,128)} %sx_in.1) | copy-start | bytes 49156
  0.7 28.4 %copy-start.4 = (f32[16,256]{1,0:T(8,128)S(1)}, f32[16,256]{1,0:T(8,128)}, u32[]{:S(2)}) copy-start(f32[16,256]{1,0:T(8,128)} %sy_in.1) | copy-start | bytes 49156
  0.7 28.4 %copy-start.5 = (f32[48,48]{1,0:T(8,128)S(1)}, f32[48,48]{1,0:T(8,128)}, u32[]{:S(2)}) copy-start(f32[48,48]{1,0:T(8,128)} %constant.8.clone.halo_in) | copy-start | bytes 27652
  0.7 28.4 %copy-start.6 = (f32[48,48]{1,0:T(8,128)S(1)}, f32[48,48]{1,0:T(8,128)}, u32[]{:S(2)}) copy-start(f32[48,48]{1,0:T(8,128)} %constant.7.clone.own_in) | copy-start | bytes 27652

commit v7 on v6

--- a/solution.py
+++ b/solution.py
@@ -972,7 +972,7 @@
 
         low, high = converted(c)
         lax.fori_loop(0, levels * (high - low), convert(low, high - low), 0, unroll=2 * (high - low))
-        for k in range(1, n_tm):
+        for k in sorted(range(1, n_tm), key=lambda k: abs(k - n_tm // 2)):
             part_copy(c, k, t).start()
 
     def narrow(s, carry):

time: 30.6 us -> 30.6 us (level)
  no operation moved by 1% of the time
where the time goes in v7:
time: 30.6 us; the launch traced here: 30.5 us
  Pallas kernels  28.6 us (93%)
  between operations  1.56 us (5%)
    pallas_call x1, Pallas kernels, quick(): pl.pallas_call(functools.partial(fast_kernel, n_tm, n_tile, levels), out_...  27.7 us
    pallas_call x1, Pallas kernels, store(): pl.pallas_call(store_kernel, out_shape=(jax.ShapeDtypeStruct(a.shape, a.d...  0.9 us

profile of v7, /device:TPU:0, one launch (start us, length us, event | category | flops | bytes accessed | tf_op | source)
XLA Modules:
  0.0 30.5 jit_solution(16375765000166957624)
XLA Ops:
  0.6 0.0 copy-start
  0.6 0.0 copy-start.1
  0.7 0.0 copy-start.2
  0.7 0.0 copy-start.3
  0.7 0.0 copy-start.4
  0.7 0.0 copy-start.5
  0.7 0.0 copy-start.6
  0.7 27.7 %shard_map.95 = (bf16[48,32,256]{2,1,0:T(8,128)(2,1)S(1)}, f32[2,16,256]{2,1,0:T(8,128)S(1)}, f32[1]{0:T(128)}) custom-call(f32[48,32,256]{2,1,0:T(8,128)} %bitcast.4, f32[48,32,256]{2,1,0:T(8,128)} %bitcast.6, s32[16,256]{1,0:T(8,128)} %land_in.1, s32[16,256]{1,0:T(8,128)} %bottom_in.1, f32[16,256]{1,0:T(8,128)} %sx_in.1, f32[16,256]{1,0:T(8,128)} %sy_in.1, ...), custom_call_target="tpu_custom_call" | custom-call | flops 1000000000 | bytes 4000000 | tf_op jit(solution)/shard_map/pallas_call | solution.py:1097
  29.1 0.0 copy-done
  29.1 0.0 copy-done.1
  29.1 0.0 copy-done.2
  29.1 0.0 copy-done.3
  29.1 0.0 copy-done.4
  29.1 0.0 copy-done.5
  29.1 0.0 copy-done.6
  29.1 0.2 conditional.1
  29.4 0.9 %store.1 = (bf16[48,32,256]{2,1,0:T(8,128)(2,1)}, f32[2,16,256]{2,1,0:T(8,128)}) custom-call(bf16[48,32,256]{2,1,0:T(8,128)(2,1)S(1)} %get-tuple-element.40.a_ref, f32[2,16,256]{2,1,0:T(8,128)S(1)} %get-tuple-element.41.b_ref), custom_call_target="tpu_custom_call" | custom-call | tf_op jit(solution)/shard_map/store/pallas_call | solution.py:1192
Async XLA Ops:
  0.6 28.4 %copy-start = (f32[48,2,16,256]{3,2,1,0:T(8,128)S(1)}, f32[48,2,16,256]{3,2,1,0:T(8,128)}, u32[]{:S(2)}) copy-start(f32[48,2,16,256]{3,2,1,0:T(8,128)} %param.10) | copy-start | bytes 4718596
  0.6 28.4 %copy-start.1 = (s32[16,256]{1,0:T(8,128)S(1)}, s32[16,256]{1,0:T(8,128)}, u32[]{:S(2)}) copy-start(s32[16,256]{1,0:T(8,128)} %land_in.1) | copy-start | bytes 49156
  0.7 28.4 %copy-start.2 = (s32[16,256]{1,0:T(8,128)S(1)}, s32[16,256]{1,0:T(8,128)}, u32[]{:S(2)}) copy-start(s32[16,256]{1,0:T(8,128)} %bottom_in.1) | copy-start | bytes 49156
  0.7 28.4 %copy-start.3 = (f32[16,256]{1,0:T(8,128)S(1)}, f32[16,256]{1,0:T(8,128)}, u32[]{:S(2)}) copy-start(f32[16,256]{1,0:T(8,128)} %sx_in.1) | copy-start | bytes 49156
  0.7 28.4 %copy-start.4 = (f32[16,256]{1,0:T(8,128)S(1)}, f32[16,256]{1,0:T(8,128)}, u32[]{:S(2)}) copy-start(f32[16,256]{1,0:T(8,128)} %sy_in.1) | copy-start | bytes 49156
  0.7 28.4 %copy-start.5 = (f32[48,48]{1,0:T(8,128)S(1)}, f32[48,48]{1,0:T(8,128)}, u32[]{:S(2)}) copy-start(f32[48,48]{1,0:T(8,128)} %constant.8.clone.halo_in) | copy-start | bytes 27652
  0.7 28.4 %copy-start.6 = (f32[48,48]{1,0:T(8,128)S(1)}, f32[48,48]{1,0:T(8,128)}, u32[]{:S(2)}) copy-start(f32[48,48]{1,0:T(8,128)} %constant.7.clone.own_in) | copy-start | bytes 27652
